TPU v7x, 256 devices: a whole 4x4x8 slice. The times are simulated.
256 devices in a mesh: dp: 8 (over z_hi, x), ep: 8 (over y, core), ctx: 4 (over z_lo).
Axes of the slice: x: 4, y: 4, z: 8 (z_hi: 2, z_lo: 4; z = z_hi * 4 + z_lo), core: 2. Of those that a mesh axis runs over, the one named last changes fastest.
Arguments:
- layer_input: bfloat16 [32768, 1024], P(('dp', 'ep', 'ctx')), may hold values from -24 to 24
- gain_attn: float32 [1024], replicated, may hold values from 0.5 to 1.5
- w_query: bfloat16 [1024, 1024], replicated, may hold values from -0.1875 to 0.1875
- w_key: bfloat16 [1024, 512], replicated, may hold values from -0.1875 to 0.1875
- w_value: bfloat16 [1024, 512], replicated, may hold values from -0.1875 to 0.1875
- w_proj: bfloat16 [1024, 1024], replicated, may hold values from -1 to 1
- gain_ffn: float32 [1024], replicated, may hold values from 0.5 to 1.5
- w_router: bfloat16 [1024, 32], replicated, may hold values from -0.09375 to 0.09375
- w_expert_in: bfloat16 [32, 1024, 1024], P('ep'), may hold values from -0.1875 to 0.1875
- w_expert_out: bfloat16 [32, 512, 1024], P('ep'), may hold values from -1 to 1
- segment_ids: int32 [8, 4096], P('dp'), may hold values from 0 to 127, never falling along the last dimension, each value on 1 to 3072 neighbouring positions
- expert_ids: int32 [32768, 8], P(('dp', 'ep', 'ctx')), may hold values from 0 to 31, all different within a row
- slot_order: int32 [256, 1024], P(('dp', 'ep', 'ctx')), may hold values from 0 to 1023, each once within a row
- out_grad: bfloat16 [32768, 1024], P(('dp', 'ep', 'ctx')), may hold values from -6 to 6
Outputs:
- layer_output: bfloat16 [32768, 1024], P(('dp', 'ep', 'ctx'))
- input_grad: bfloat16 [32768, 1024], P(('dp', 'ep', 'ctx'))
- grad_gain_attn: float32 [1024], P(('dp', 'ep', 'ctx'))
- grad_query: float32 [1024, 1024], P(('dp', 'ep', 'ctx'))
- grad_key: float32 [1024, 512], P(('dp', 'ep', 'ctx'))
- grad_value: float32 [1024, 512], P(('dp', 'ep', 'ctx'))
- grad_proj: float32 [1024, 1024], P(('dp', 'ep', 'ctx'))
- grad_gain_ffn: float32 [1024], P(('dp', 'ep', 'ctx'))
- grad_router: float32 [1024, 32], P(('dp', 'ep', 'ctx'))
- grad_expert_in: float32 [32, 1024, 1024], P('ep', ('dp', 'ctx'))
- grad_expert_out: float32 [32, 512, 1024], P('ep', ('dp', 'ctx'))
Inputs may be any that keep to these rules, and one draw needn't show every extreme that they name: `segment_ids`: within a sequence the ids never fall; each document is at most 3072 tokens long and one is exactly that long. `expert_ids`: each row names 8 different experts. `slot_order`: each row holds every number below 1024 once.
All inputs are finite; a program needn't handle non-finite values.
Results may differ from a plain program's by a relative error of at most 0.025.
Values may be sent and summed in bfloat16 or wider, within the bound.
A program may use at most 192 MiB of HBM per device.

v0:
```python
from functools import partial

import jax
import jax.numpy as jnp
import numpy as np
from jax import lax
from jax.experimental import pallas as pl
from jax.experimental.pallas import tpu as pltpu
from jax.sharding import PartitionSpec as P

HD = 64
EPSILON = 1e-06
MASKED = -1e30
CAP = 40
TOK = 128
BIG = 4096.0
MESH = pl.DeviceIdType.MESH
F32 = jnp.float32
BF16 = jnp.bfloat16
VMEM_LIMIT = 60 * 1024 * 1024

NT = (((1,), (1,)), ((), ()))
NN = (((1,), (0,)), ((), ()))
TN = (((0,), (0,)), ((), ()))


def mm(a, b, dims=NN):
    return lax.dot_general(a, b, dims, preferred_element_type=F32)


def mm3(a, b, dims=NN):
    high = a.astype(BF16)
    low = (a - high.astype(F32)).astype(BF16)
    return mm(high, b, dims) + mm(low, b, dims)


def where_am_i():
    dp, ep, ctx = lax.axis_index("dp"), lax.axis_index("ep"), lax.axis_index("ctx")
    return dp, ep, ctx


def remote(src, dst, send, recv, device):
    return pltpu.make_async_remote_copy(
        src_ref=src, dst_ref=dst, send_sem=send, recv_sem=recv, device_id=device, device_id_type=MESH
    )


def greet(barrier, device):
    pl.semaphore_signal(barrier, inc=1, device_id=device, device_id_type=MESH)


def rotate_half(values):
    lane = lax.broadcasted_iota(jnp.int32, values.shape, 1)
    return jnp.where(lane % HD < HD // 2, pltpu.roll(values, 96, 1), pltpu.roll(values, 32, 1))


def rope_block(block, ca_ref, sa_ref, cb_ref, sb_ref):
    ca, sa = ca_ref[pl.ds(block, 1), :], sa_ref[pl.ds(block, 1), :]
    cb, sb = cb_ref[...], sb_ref[...]
    cosine = ca * cb - sa * sb
    sine = sa * cb + ca * sb
    lane = lax.broadcasted_iota(jnp.int32, cosine.shape, 1)
    return cosine, jnp.where(lane % HD < HD // 2, -sine, sine)


def rope_tables():
    frequency = 10000.0 ** (-np.arange(HD // 2, dtype=np.float64) * 2.0 / HD)
    frequency = np.tile(frequency.astype(np.float32).astype(np.float64), 4)
    blocks = np.arange(32, dtype=np.float64)[:, None] * 128.0 * frequency[None, :]
    rows = np.arange(128, dtype=np.float64)[:, None] * frequency[None, :]
    return [t.astype(np.float32) for t in (np.cos(blocks), np.sin(blocks), np.cos(rows), np.sin(rows))]


class EpGather:
    COUNT = 13

    def __init__(self, ref, send, recv, place):
        self.ref, self.send, self.recv = ref, send, recv
        dp, ep, ctx = place
        y, k = ep // 2, ep % 2
        self.up = (dp, ((y + 1) % 4) * 2 + k, ctx)
        self.dn = (dp, ((y + 3) % 4) * 2 + k, ctx)
        self.sib = (dp, y * 2 + 1 - k, ctx)

        def at(dy, other):
            return ((y + dy) % 4) * 2 + ((1 - k) if other else k)

        u, s, d = self.up, self.sib, self.dn
        self.sends = [
            (at(0, 0), None, s), (at(0, 0), 0, u), (at(0, 0), 1, u), (at(0, 0), 1, d), (at(0, 0), 0, d),
            (at(3, 0), 0, u), (at(3, 0), 0, s), (at(1, 0), 1, d), (at(1, 0), 1, s),
            (at(3, 0), 1, s), (at(1, 0), 0, s), (at(2, 0), 0, s), (at(2, 0), 1, s),
        ]
        self.gets = [
            (at(0, 1), None), (at(3, 0), 0), (at(3, 0), 1), (at(1, 0), 1), (at(1, 0), 0),
            (at(2, 0), 0), (at(3, 1), 0), (at(2, 0), 1), (at(1, 1), 1),
            (at(3, 1), 1), (at(1, 1), 0), (at(2, 1), 0), (at(2, 1), 1),
        ]

    def view(self, block, half):
        if half is None:
            return self.ref.at[block]
        rows = self.ref.shape[1] // 2
        return self.ref.at[block, pl.ds(half * rows, rows)]

    def go(self, *which):
        for i in which:
            block, half, device = self.sends[i]
            v = self.view(block, half)
            remote(v, v, self.send.at[i], self.recv.at[i], device).start()

    def got(self, *which):
        for i in which:
            v = self.view(*self.gets[i])
            remote(v, v, self.send.at[i], self.recv.at[i], self.sends[i][2]).wait_recv()

    def sent(self):
        for i in range(self.COUNT):
            block, half, device = self.sends[i]
            v = self.view(block, half)
            remote(v, v, self.send.at[i], self.recv.at[i], device).wait_send()

    def whole(self):
        self.got(1)
        self.go(5, 6)
        self.got(3)
        self.go(7, 8)
        self.got(2)
        self.go(9)
        self.got(4)
        self.go(10)
        self.got(5)
        self.go(11)
        self.got(7)
        self.go(12)
        self.got(0, 6, 8, 9, 10, 11, 12)


class EpScatterSum:
    COUNT = 8

    def __init__(self, part, cbuf, fbuf, gbuf, send, recv, place):
        self.part, self.cbuf, self.fbuf, self.gbuf = part, cbuf, fbuf, gbuf
        self.send, self.recv = send, recv
        dp, ep, ctx = place
        self.y, self.k = ep // 2, ep % 2
        y, k = self.y, self.k
        self.up = (dp, ((y + 1) % 4) * 2 + k, ctx)
        self.dn = (dp, ((y + 3) % 4) * 2 + k, ctx)
        self.sib = (dp, y * 2 + 1 - k, ctx)

    def block(self, dy, other=False):
        return ((self.y + dy) % 4) * 2 + ((1 - self.k) if other else self.k)

    def copy(self, i):
        half = self.cbuf.shape[1] // 2
        lo, hi = pl.ds(0, half), pl.ds(half, half)
        s, r = self.send, self.recv
        if i < 4:
            away = self.block((2, 1, 3, 0)[i], True)
            return remote(self.part.at[away], self.cbuf.at[i], s.at[i], r.at[i], self.sib)
        src, dst, device = (
            (self.cbuf.at[0, lo], self.fbuf.at[0], self.up),
            (self.cbuf.at[0, hi], self.fbuf.at[1], self.dn),
            (self.cbuf.at[1], self.gbuf.at[0], self.up),
            (self.cbuf.at[2], self.gbuf.at[1], self.dn),
        )[i - 4]
        return remote(src, dst, s.at[i], r.at[i], device)

    def start(self):
        for i in range(4):
            self.copy(i).start()

    def far(self):
        self.copy(0).wait_recv()
        self.cbuf[0] = (self.cbuf[0].astype(F32) + self.part[self.block(2)].astype(F32)).astype(BF16)
        self.copy(4).start()
        self.copy(5).start()

    def near(self):
        half = self.cbuf.shape[1] // 2
        for slot, dy, far, rows, rest in ((1, 1, 0, pl.ds(0, half), pl.ds(half, half)), (2, 3, 1, pl.ds(half, half), pl.ds(0, half))):
            b = self.block(dy)
            self.copy(slot).wait_recv()
            self.copy(4 + far).wait_recv()
            self.cbuf[slot, rows] = (
                self.cbuf[slot, rows].astype(F32) + self.part[b, rows].astype(F32) + self.fbuf[far].astype(F32)
            ).astype(BF16)
            self.cbuf[slot, rest] = (self.cbuf[slot, rest].astype(F32) + self.part[b, rest].astype(F32)).astype(BF16)
            self.copy(6 + far).start()

    def last(self):
        for i in (3, 6, 7):
            self.copy(i).wait_recv()
        return (
            self.part[self.block(0)].astype(F32) + self.cbuf[3].astype(F32)
            + self.gbuf[0].astype(F32) + self.gbuf[1].astype(F32)
        )

    def sent(self):
        for i in range(self.COUNT):
            self.copy(i).wait_send()


def scatter_sum_scratch():
    return [
        pltpu.VMEM((4, TOK, 1024), BF16),
        pltpu.VMEM((2, TOK // 2, 1024), BF16),
        pltpu.VMEM((2, TOK, 1024), BF16),
        pltpu.SemaphoreType.DMA((8,)),
        pltpu.SemaphoreType.DMA((8,)),
    ]


def repeat(first, last, work):
    def each(i, carry):
        work(i)
        return carry

    lax.fori_loop(first, last, each, 0)


def exchange(src, dst, send, recv, place, wait):
    dp, ep, ctx = place

    def one(r):
        to, source = (ep + r) % 8, (ep + 8 - r) % 8
        if not wait:
            remote(src.at[to], dst.at[ep], send.at[r], recv.at[r], (dp, to, ctx)).start()
        else:
            remote(src.at[to], dst.at[source], send.at[r], recv.at[r], (dp, to, ctx)).wait_recv()

    repeat(1, 8, one)


def exchange_sent(src, dst, send, recv, place):
    dp, ep, ctx = place

    def one(r):
        to = (ep + r) % 8
        remote(src.at[to], dst.at[ep], send.at[r], recv.at[r], (dp, to, ctx)).wait_send()

    repeat(1, 8, one)


def starts_of(docs):
    rows = lax.broadcasted_iota(jnp.int32, docs.shape, 0)
    lane = lax.broadcasted_iota(jnp.int32, docs.shape, 1)
    docs = docs.astype(F32)
    turned = pltpu.roll(docs, 1, 1)
    before = jnp.where(lane == 0, pltpu.roll(turned, 1, 0), turned)
    place = rows * 128 + lane
    fresh = (docs != before) | (place == 0)
    value = jnp.where(fresh, place.astype(F32), 0.0)
    for shift in (1, 2, 4, 8, 16, 32, 64):
        value = jnp.maximum(value, jnp.where(lane >= shift, pltpu.roll(value, shift, 1), 0.0))
    carry = jnp.broadcast_to(jnp.max(value, axis=1, keepdims=True), value.shape)
    for shift in (1, 2, 4, 8, 16):
        carry = jnp.maximum(carry, jnp.where(rows >= shift, pltpu.roll(carry, shift, 0), 0.0))
    above = jnp.where(rows >= 1, pltpu.roll(carry, 1, 0), 0.0)
    return jnp.maximum(value, above)


def slots_of(eid_ref, eidT_ref, so_ref, soT_ref, slot_scr, sel_ref):
    def expert(index):
        return jnp.where(index % 8 < 4, (index // 8) * 4 + index % 8, -1)

    row_expert = expert(lax.broadcasted_iota(jnp.int32, (64, TOK), 0))
    lane_expert = expert(lax.broadcasted_iota(jnp.int32, (TOK, 64), 1))
    by_row = jnp.full((64, TOK), BIG, F32)
    by_lane = jnp.full((TOK, 64), BIG, F32)
    for k in range(8):
        by_row = jnp.where(eidT_ref[k : k + 1, :] == row_expert, soT_ref[k : k + 1, :].astype(F32), by_row)
        by_lane = jnp.where(eid_ref[:, k : k + 1] == lane_expert, so_ref[:, k : k + 1].astype(F32), by_lane)
    sel_ref[...] = jnp.where(by_row < BIG, 1.0, 0.0)
    for g in range(8):
        for j in range(4):
            r = 8 * g + j
            row = by_row[r : r + 1, :]
            less = jnp.where(by_lane[:, r : r + 1] < row, 1.0, 0.0)
            rank = jnp.sum(less, axis=0, keepdims=True)
            slot_scr[g, j : j + 1, :] = jnp.where((row < BIG) & (rank < CAP), rank, -1.0)
        slot_scr[g, 4:8, :] = jnp.full((4, TOK), -1.0, F32)


def first_kernel(
    x_ref, gain_ref, og_ref, w_ref, ca_ref, sa_ref, cb_ref, sb_ref, eid_ref, eidT_ref, so_ref, soT_ref, doc_ref,
    nall_ref, q_ref, kv_ref, ogall_ref, slot_ref, sel_ref, start_ref,
    slot_scr, nsend, nrecv, osend, orecv, ssend, srecv, ksend, krecv,
):
    place = where_am_i()
    dp, ep, ctx = place
    y = ep // 2
    barrier = pltpu.get_barrier_semaphore()
    for r in range(1, 8):
        greet(barrier, (dp, (ep + r) % 8, ctx))

    @pl.when(ctx > 0)
    def _():
        greet(barrier, (dp, ep, ctx - 1))

    @pl.when(ctx < 3)
    def _():
        greet(barrier, (dp, ep, ctx + 1))

    x = x_ref[...].astype(F32)
    normed = x * lax.rsqrt(jnp.mean(x * x, axis=-1, keepdims=True) + EPSILON) * gain_ref[...]
    nall_ref[ep] = normed.astype(BF16)
    ogall_ref[ep] = og_ref[...]
    edges = jnp.where(ctx > 0, 1, 0) + jnp.where(ctx < 3, 1, 0)
    pl.semaphore_wait(barrier, 7 + edges)

    gather = EpGather(nall_ref, nsend, nrecv, place)
    grads = EpGather(ogall_ref, osend, orecv, place)
    gather.go(0, 1, 3, 2, 4)

    start_ref[...] = starts_of(doc_ref[...])
    slots_of(eid_ref, eidT_ref, so_ref, soT_ref, slot_scr, sel_ref)
    slot_ref[ep] = slot_scr[ep]
    exchange(slot_scr, slot_ref, ssend, srecv, place, False)

    lane = lax.broadcasted_iota(jnp.int32, (TOK, 128), 1)

    def project(dy):
        chip = (y + dy) % 4
        rows = jnp.concatenate([nall_ref[2 * chip], nall_ref[2 * chip + 1]], axis=0)
        out = mm(rows, w_ref[...])
        for i in range(2):
            b = 2 * chip + i
            cosine, sine = rope_block(4 * b + ctx, ca_ref, sa_ref, cb_ref, sb_ref)
            q = out[i * TOK : (i + 1) * TOK, :128]
            kv = out[i * TOK : (i + 1) * TOK, 128:]
            q_rot = (q * cosine + rotate_half(q) * sine).astype(BF16)
            q_ref[b] = (q_rot.astype(F32) * (HD**-0.5)).astype(BF16)
            cosine = jnp.where(lane < HD, cosine, 1.0)
            sine = jnp.where(lane < HD, sine, 0.0)
            kv_ref[b, ctx] = (kv * cosine + rotate_half(kv) * sine).astype(BF16)

    offsets = (0, 3, 1, 2)

    def hop(direction, h, g, action):
        chip = (y + offsets[g]) % 4
        back = h - 1
        own = ctx - back if direction == 0 else ctx + back
        come = ctx - h if direction == 0 else ctx + h
        to = ctx + 1 if direction == 0 else ctx - 1
        index = (direction * 3 + back) * 4 + g
        send, recv = ksend.at[index], krecv.at[index]
        if action == "recv":
            ok = come >= 0 if direction == 0 else come <= 3

            @pl.when(ok)
            def _():
                v = kv_ref.at[pl.ds(2 * chip, 2), come]
                remote(v, v, send, recv, (dp, ep, ctx)).wait_recv()

        else:
            ok = (own >= 0) & (ctx < 3) if direction == 0 else (own <= 3) & (ctx > 0)

            @pl.when(ok)
            def _():
                v = kv_ref.at[pl.ds(2 * chip, 2), own]
                c = remote(v, v, send, recv, (dp, ep, to))
                c.start() if action == "send" else c.wait_send()

    def hops(h, g):
        for direction in (0, 1):
            if h > 1:
                hop(direction, h - 1, g, "recv")
            hop(direction, h, g, "send")

    gather.got(0)
    project(0)
    hops(1, 0)
    gather.got(1)
    gather.go(5, 6)
    gather.got(3)
    gather.go(7, 8)
    gather.got(2)
    gather.go(9)
    gather.got(4)
    gather.go(10)
    grads.go(0, 1, 3, 2, 4)
    gather.got(6, 9)
    project(3)
    hops(1, 1)
    hops(2, 0)
    gather.got(8, 10)
    project(1)
    hops(1, 2)
    hops(2, 1)
    hops(3, 0)
    gather.got(5)
    gather.go(11)
    gather.got(7)
    gather.go(12)
    gather.got(11, 12)
    project(2)
    hops(1, 3)
    hops(2, 2)
    hops(3, 1)
    hops(2, 3)
    hops(3, 2)
    grads.whole()
    hops(3, 3)
    for g in range(4):
        for direction in (0, 1):
            hop(direction, 3, g, "recv")
    exchange(slot_scr, slot_ref, ssend, srecv, place, True)
    gather.sent()
    grads.sent()
    exchange_sent(slot_scr, slot_ref, ssend, srecv, place)
    for g in range(4):
        for h in (1, 2, 3):
            for direction in (0, 1):
                hop(direction, h, g, "sent")


CHUNK = 512


def key_mask(chunk, start_row, place_row):
    keys = (lax.broadcasted_iota(jnp.int32, (CHUNK, 256), 0) + chunk * CHUNK).astype(F32)
    return (keys >= start_row) & (keys <= place_row)


def query_rows(j, ctx, start_ref):
    block = 4 * j + ctx
    start = start_ref[pl.ds(block, 1), :]
    places = (lax.broadcasted_iota(jnp.int32, (1, 128), 1) + block * 128).astype(F32)
    return jnp.concatenate([start, start], axis=1), jnp.concatenate([places, places], axis=1)


def turned(block):
    return block.astype(F32).T.astype(BF16)


def heads_wide(tall):
    return jnp.concatenate([tall[:HD], tall[HD:]], axis=1)


def attend_kernel(first_ref, q_ref, kv_ref, start_ref, att_ref, attT_ref, lse_ref, kvT):
    ctx = lax.axis_index("ctx")

    for chunk in range(8):
        part = kv_ref[chunk * CHUNK : (chunk + 1) * CHUNK, :].astype(F32).T
        row = lax.broadcasted_iota(jnp.int32, part.shape, 0)
        kvT[:, chunk * CHUNK : (chunk + 1) * CHUNK] = jnp.where(row < HD, 1.0, part).astype(BF16)

    for j in range(8):
        start_row, place_row = query_rows(j, ctx, start_ref)
        wide = heads_wide(turned(q_ref[j]))
        q_pad = jnp.concatenate([wide, jnp.zeros_like(wide)], axis=0)

        def step(chunk, carry):
            top, total = carry
            rows = pl.ds(pl.multiple_of(chunk * CHUNK, CHUNK), CHUNK)
            scores = mm(kv_ref[rows, :], q_pad)
            scores = jnp.where(key_mask(chunk, start_row, place_row), scores, MASKED)
            new_top = jnp.maximum(top, jnp.max(scores, axis=0, keepdims=True))
            probs = jnp.exp(scores - new_top).astype(BF16)
            total = total * jnp.exp(top - new_top) + mm(kvT[:, rows], probs)
            return new_top, total

        top, total = lax.fori_loop(
            first_ref[j], j + 1, step, (jnp.full((1, 256), MASKED, F32), jnp.zeros((128, 256), F32))
        )
        norm = total[0:1]
        out = total[HD:] / norm
        tall = jnp.concatenate([out[:, :128], out[:, 128:]], axis=0)
        attT_ref[j] = tall
        att_ref[j] = tall.T.astype(BF16)
        lse_ref[j] = jnp.broadcast_to(top + jnp.log(norm), (8, 256))


def middle_kernel(
    att_ref, x_ref, gain_ref, w_ref, wr_ref, sel_ref,
    res_ref, nf_ref, gin_ref, gates_ref,
    abuf, gscr, asend, arecv, nsend, nrecv, gsend, grecv,
):
    place = where_am_i()
    dp, ep, ctx = place
    barrier = pltpu.get_barrier_semaphore()
    for r in range(1, 8):
        greet(barrier, (dp, (ep + r) % 8, ctx))
    pl.semaphore_wait(barrier, 7)
    exchange(att_ref, abuf, asend, arecv, place, False)
    abuf[ep] = att_ref[ep]
    exchange(att_ref, abuf, asend, arecv, place, True)
    attended = jnp.concatenate([abuf[p] for p in range(8)], axis=1)
    res = x_ref[...].astype(F32) + mm(attended, w_ref[...])
    res_ref[...] = res
    normed = res * lax.rsqrt(jnp.mean(res * res, axis=-1, keepdims=True) + EPSILON) * gain_ref[...]
    normed = normed.astype(BF16)
    nf_ref[ep] = normed
    gather = EpGather(nf_ref, nsend, nrecv, place)
    gather.go(0, 1, 3, 2, 4)
    logits = mm(wr_ref[...], normed, NT)
    chosen = sel_ref[...] > 0.5
    top = jnp.max(jnp.where(chosen, logits, MASKED), axis=0, keepdims=True)
    weight = jnp.where(chosen, jnp.exp(jnp.where(chosen, logits, MASKED) - top), 0.0)
    gates = weight / jnp.sum(weight, axis=0, keepdims=True)
    gates_ref[...] = gates
    for g in range(8):
        gscr[g] = gates[8 * g : 8 * g + 8, :]
    gin_ref[ep] = gscr[ep]
    exchange(gscr, gin_ref, gsend, grecv, place, False)
    gather.whole()
    exchange(gscr, gin_ref, gsend, grecv, place, True)
    gather.sent()
    exchange_sent(gscr, gin_ref, gsend, grecv, place)
    exchange_sent(att_ref, abuf, asend, arecv, place)


def each_slab(lead, work):
    count = 1
    for size in lead:
        count *= size

    def each(i, carry):
        work((i,) if len(lead) == 1 else (i // lead[1], i % lead[1]))
        return carry

    lax.fori_loop(0, count, each, 0)


class Arc:
    def __init__(self, n, pos, own, half, slots, devices, send, recv):
        self.n, self.pos, self.own, self.half, self.slots = n, pos, own, half, slots
        self.devices, self.send, self.recv = devices, send, recv
        self.steps = n // 2

    def chunk(self, way, s):
        reach = self.steps - s + 1
        return (self.pos + reach) % self.n if way == 0 else (self.pos + self.n - reach) % self.n

    def copy(self, way, s):
        dst = self.slots.at[way, s - 1]
        src = self.own(self.chunk(way, s)) if s == 1 else self.slots.at[way, s - 2]
        if s == 1:
            src, dst = self.half(src, way), self.half(dst, way)
        return remote(src, dst, self.send.at[way, s - 1], self.recv.at[way, s - 1], self.devices[way])

    def start(self):
        for way in (0, 1):
            self.copy(way, 1).start()

    def slabs(self, work):
        each_slab(self.slots.shape[2:-2], work)

    def advance(self, s):
        for way in (0, 1):
            self.copy(way, s - 1).wait_recv()
            held, own = self.slots.at[way, s - 2], self.own(self.chunk(way, s))
            if s == 2:
                self.merge(way, held, own)
            else:

                def add(index):
                    held[index] = (held[index].astype(F32) + own[index].astype(F32)).astype(BF16)

                self.slabs(add)
            self.copy(way, s).start()

    def merge(self, way, held, own):
        mine, its = self.half(held, way), self.half(own, way)
        other, from_own = self.half(held, 1 - way), self.half(own, 1 - way)

        def add(index):
            mine[index] = (mine[index].astype(F32) + its[index].astype(F32)).astype(BF16)

        def take(index):
            other[index] = from_own[index]

        each_slab(mine.shape[:-2], add)
        each_slab(other.shape[:-2], take)

    def finish(self, put):
        for way in (0, 1):
            self.copy(way, self.steps).wait_recv()
        own, up, down = self.own(self.pos), self.slots.at[0, self.steps - 1], self.slots.at[1, self.steps - 1]

        def add(index):
            put(index, own[index].astype(F32) + up[index].astype(F32) + down[index].astype(F32))

        self.slabs(add)

    def sent(self):
        for way in (0, 1):
            for s in range(1, self.steps + 1):
                self.copy(way, s).wait_send()


class Torus:
    def __init__(self, place):
        self.dp, self.ep, self.ctx = place
        self.zh, self.x = self.dp // 4, self.dp % 4
        self.z = self.zh * 4 + self.ctx

    def at_x(self, v):
        return (self.zh * 4 + v % 4, self.ep, self.ctx)

    def at_z(self, v):
        v = v % 8
        return ((v // 4) * 4 + self.x, self.ep, v % 4)

    def x_ways(self):
        return self.at_x(self.x + 1), self.at_x(self.x + 3)

    def z_ways(self):
        return self.at_z(self.z + 1), self.at_z(self.z + 7)

    def x_arc(self, own, half, slots, send, recv):
        return Arc(4, self.x, own, half, slots, self.x_ways(), send, recv)

    def z_arc(self, own, half, slots, send, recv):
        return Arc(8, self.z, own, half, slots, self.z_ways(), send, recv)


def first_or_last(sizes):
    def half(view, h):
        return view.at[pl.ds(0, sizes[0])] if h == 0 else view.at[pl.ds(sizes[0], sizes[1])]

    return half


X_FIRST, Z_FIRST = (0, 1), (2,)
KEPT = 3
X_UNITS, Z_UNITS = (3, 4, 5, 6, 7, 8, 9), (10, 11)


def unit_arcs(torus, own, x_units, z_units, x_slots, z_slots, xs, xr, zs, zr):
    xa = [
        torus.x_arc(
            lambda t, i=i: own.at[i, :, t], first_or_last((1, 1)), x_slots.at[i], xs.at[i], xr.at[i]
        )
        for i in range(len(x_units))
    ]
    za = [
        torus.z_arc(
            lambda t, i=i: own.at[len(x_units) + i, t // 4, :, t % 4], first_or_last((2, 2)), z_slots.at[i], zs.at[i], zr.at[i]
        )
        for i in range(len(z_units))
    ]
    return xa, za


def expert_kernel(
    slot_ref, gate_ref, nf_hbm, og_hbm, win_hbm, wout_hbm,
    y_ref, d_ref, dg_ref, rx_ref, rz_ref, gw_hbm,
    nf, og, win, wout, rows_scr, grad_scr, units, x_slots, z_slots,
    fsem, wsem, gsem, xs, xr, zs, zr,
):
    torus = Torus(where_am_i())
    loads = [pltpu.make_async_copy(nf_hbm, nf, fsem.at[0]), pltpu.make_async_copy(og_hbm, og, fsem.at[1])]

    def weights(j):
        return (
            pltpu.make_async_copy(win_hbm.at[j], win.at[j % 2], wsem.at[j, 0]),
            pltpu.make_async_copy(wout_hbm.at[j], wout.at[j % 2], wsem.at[j, 1]),
        )

    for f in loads + list(weights(0)) + list(weights(1)):
        f.start()
    barrier = pltpu.get_barrier_semaphore()
    for device in torus.x_ways() + torus.z_ways():
        greet(barrier, device)
    slot = lax.broadcasted_iota(jnp.int32, (CAP, TOK), 0).astype(F32)

    def picks(s, e):
        return slot == slot_ref[s, pl.ds(e, 1), :]

    for f in loads:
        f.wait()

    def load(s, carry):
        pick = jnp.concatenate([jnp.where(picks(s, e), 1.0, 0.0) for e in range(4)], axis=0).astype(BF16)
        got = mm(pick, nf[s])
        grad = mm(pick, og[s])
        for e in range(4):
            rows = pl.ds(pl.multiple_of(s * CAP, 8), CAP)
            rows_scr[e, rows, :] = got[e * CAP : (e + 1) * CAP]
            grad_scr[e, rows, :] = grad[e * CAP : (e + 1) * CAP]
        return carry

    lax.fori_loop(0, 8, load, 0)

    xa, za = unit_arcs(torus, units, X_FIRST, Z_FIRST, x_slots, z_slots, xs, xr, zs, zr)
    views = (2, 4, 4, 16, 1024)

    def back_weights(j, received, grad_gu):
        grad_in = mm(received, grad_gu, TN).astype(BF16).reshape(32, 32, 1024)
        units[3 * j] = grad_in[:, 0:16].reshape(views)
        units[3 * j + 1] = grad_in[:, 16:32].reshape(views)

    def expert(j, carry):
        gates = jnp.concatenate(
            [
                jnp.sum(jnp.where(picks(s, j), gate_ref[s, pl.ds(j, 1), :], 0.0), axis=1, keepdims=True)
                for s in range(8)
            ],
            axis=0,
        )
        for f in weights(j):
            f.wait()
        w_in, w_out = win[j % 2], wout[j % 2]
        received = rows_scr[j].astype(BF16)
        grad_tok = grad_scr[j]
        gate_up = mm(received, w_in)
        gating, up = gate_up[:, :512], gate_up[:, 512:]
        sig = 1.0 / (1.0 + jnp.exp(-gating))
        silu = gating * sig
        act = (silu * up).astype(BF16)
        result = mm(act, w_out).astype(BF16).astype(F32)
        dots = jnp.sum(grad_tok * result, axis=1, keepdims=True)
        grad_res = (grad_tok * gates).astype(BF16)
        grad_scr[j] = result * gates
        for s in range(8):
            dg_ref[s, pl.ds(j, 1), :] = jnp.sum(
                jnp.where(picks(s, j), dots[s * CAP : (s + 1) * CAP], 0.0), axis=0, keepdims=True
            )
        units[3 * j + 2] = mm(act, grad_res, TN).astype(BF16).reshape(views)
        grad_act = mm(grad_res, w_out, NT)
        grad_up = (grad_act * silu).astype(BF16)
        grad_gate = (grad_act * up * sig * (1.0 + gating * (1.0 - sig))).astype(BF16)
        grad_gu = jnp.concatenate([grad_gate, grad_up], axis=1)
        between(j)
        back_weights(j, received, grad_gu)
        rows_scr[j] = mm(grad_gu, w_in, NT)
        after(j)
        return carry

    def keep(first, last):
        return [pltpu.make_async_copy(units.at[u], gw_hbm.at[u - KEPT], gsem.at[u - KEPT]) for u in range(first, last)]

    def between(j):
        @pl.when(j == 1)
        def _():
            za[0].advance(2)
            xa[0].advance(2)

        @pl.when(j == 2)
        def _():
            za[0].advance(3)

        @pl.when(j == 3)
        def _():
            za[0].advance(4)

    def after(j):
        @pl.when(j < 2)
        def _():
            for f in weights(j + 2):
                f.start()

        @pl.when(j == 0)
        def _():
            for arc in za + xa:
                arc.start()

        @pl.when(j == 1)
        def _():
            xa[1].advance(2)
            for f in keep(KEPT, 6):
                f.start()

        @pl.when(j == 2)
        def _():
            for f in keep(6, 9):
                f.start()

    pl.semaphore_wait(barrier, 4)
    lax.fori_loop(0, 4, expert, 0)
    for f in keep(9, 12):
        f.start()

    def store(s, carry):
        pick = jnp.concatenate([jnp.where(picks(s, e), 1.0, 0.0) for e in range(4)], axis=0).astype(BF16)
        rows = pl.ds(pl.multiple_of(s * CAP, 8), CAP)
        weighted = jnp.concatenate([grad_scr[e, rows, :] for e in range(4)], axis=0).astype(BF16)
        y_ref[s] = mm(pick, weighted, TN).astype(BF16)
        back = jnp.concatenate([rows_scr[e, rows, :] for e in range(4)], axis=0).astype(BF16)
        d_ref[s] = mm(pick, back, TN).astype(BF16)
        dg_ref[s, 4:8, :] = jnp.zeros((4, TOK), F32)
        return carry

    lax.fori_loop(0, 8, store, 0)

    def put_z(index, value):
        for h in (0, 1):
            rz_ref[index[0], h] = value[:, 512 * h : 512 * h + 512].astype(BF16)

    za[0].finish(put_z)
    for i, arc in enumerate(xa):

        def put_x(index, value, i=i):
            rx_ref[index[0] * 4 + index[1], i] = value.astype(BF16)

        arc.finish(put_x)
    for f in keep(KEPT, 12):
        f.wait()
    for arc in xa + za:
        arc.sent()


class Direct:
    def __init__(self, torus, part, x_slots, result, z_slots, send, recv):
        self.t, self.part, self.x_slots, self.result, self.z_slots = torus, part, x_slots, result, z_slots
        self.send, self.recv = send, recv

    def x_copy(self, r):
        to = (self.t.x + r) % 4
        return remote(
            self.part.at[:, to], self.x_slots.at[r - 1], self.send.at[r], self.recv.at[r], self.t.at_x(to)
        )

    def z_copy(self, r):
        to = (self.t.z + r) % 8
        return remote(
            self.result.at[to], self.z_slots.at[r - 1], self.send.at[3 + r], self.recv.at[3 + r], self.t.at_z(to)
        )

    def start(self):
        for r in (2, 1, 3):
            self.x_copy(r).start()

    def turn(self):
        for r in (1, 2, 3):
            self.x_copy(r).wait_recv()

        def add(i, carry):
            h, l = i // 4, i % 4
            value = self.part[h, self.t.x, l].astype(F32)
            for r in range(3):
                value = value + self.x_slots[r, h, l].astype(F32)
            self.result[i] = value.astype(BF16)
            return carry

        lax.fori_loop(0, 8, add, 0)
        repeat(0, 7, lambda i: self.z_copy(4 + (2 * (i % 2) - 1) * ((i + 1) // 2)).start())

    def finish(self):
        repeat(1, 8, lambda r: self.z_copy(r).wait_recv())
        value = self.result[self.t.z].astype(F32)
        for r in range(7):
            value = value + self.z_slots[r].astype(F32)
        return value

    def sent(self):
        repeat(1, 4, lambda r: self.x_copy(r).wait_send())
        repeat(1, 8, lambda r: self.z_copy(r).wait_send())


def prepare_queries(j, ctx, start_ref, q_ref, lse_ref, both, stack, rows):
    lane = lax.broadcasted_iota(jnp.int32, (256, 128), 1)
    start_row, place_row = query_rows(j, ctx, start_ref)
    q_blk = q_ref[j]
    zero = jnp.zeros((HD, 256), BF16)
    both[j, 0:HD, 0:256] = heads_wide(turned(q_blk))
    both[j, HD:128, 0:256] = zero
    both[j, 0:HD, 256:512] = zero
    q_f = q_blk.astype(F32)
    q_rows = jnp.concatenate([q_f, pltpu.roll(q_f, HD, 1)], axis=0)
    stack[j, 0:256] = jnp.where(lane < HD, q_rows, 0.0).astype(BF16)
    rows[j, 0:1, :] = lse_ref[j, 0:1, :]
    rows[j, 2:3, :] = start_row
    rows[j, 3:4, :] = place_row


def prepare_grads(j, attT_ref, gm_ref, w_ref, both, stack, rows):
    lane = lax.broadcasted_iota(jnp.int32, (256, 128), 1)
    tall = mm(w_ref[...], gm_ref[j], NT).astype(BF16).astype(F32)
    rows[j, 1:2, :] = jnp.sum(heads_wide(tall) * heads_wide(attT_ref[j]), axis=0, keepdims=True)
    both[j, HD:128, 256:512] = heads_wide(tall).astype(BF16)
    g_f = tall.T
    g_rows = jnp.concatenate([pltpu.roll(g_f, HD, 1), g_f], axis=0)
    stack[j, 256:512] = jnp.where(lane < HD, 0.0, g_rows).astype(BF16)


def attend_pair(m, j, kv, kT, both, stack, rows):
    row = rows[j]
    chunk = pl.ds(pl.multiple_of(m * CHUNK, CHUNK), CHUNK)
    pair = mm(kv[chunk, :], both[j])
    keys = (lax.broadcasted_iota(jnp.int32, (CHUNK, 256), 0) + m * CHUNK).astype(F32)
    allowed = (keys >= row[2:3]) & (keys <= row[3:4])
    probs = jnp.exp(jnp.where(allowed, pair[:, :256], MASKED) - row[0:1])
    grad = (probs * (pair[:, 256:] - row[1:2])).astype(BF16)
    return mm(jnp.concatenate([grad, probs.astype(BF16)], axis=1), stack[j]), mm(kT[:, chunk], grad)


def tail_kernel(
    dg_ref, gates_ref, gain_two_ref, wr_ref, x_ref, gain_one_ref, ca_ref, sa_ref, cb_ref, sb_ref, start_ref, lse_ref,
    rx0, rz0,
    back_hbm, nf_hbm, res_hbm, og_hbm, q_hbm, kv_hbm, attT_hbm, wp_hbm, y_hbm, nall_hbm, wq_hbm, wk_hbm, wv_hbm, gw_hbm,
    out_ref, ing_ref, gin_ref, gout_ref, gq_ref, gk_ref, gv_ref, gside_ref, gproj_out, gains_ref,
    back, nf, res, og, q_ref, kv, attT, wp, y_part, wq, wk, wv, own,
    dbuf, cbuf, fbuf, gbuf, cbuf2, fbuf2, gbuf2, gm, gres,
    kT, both, stack, rows, dqs, acc, dkv, dqb, dkvb, kbuf, qpieces, kpieces,
    x_slots, z_slots, g0_slots, g1_slots, g2_slots, h0_slots, h1_slots, rx1, rx2, rz1,
    early, late_q, late_k, e_x, e_res, e_z, q_x, q_res, q_z, k_x, k_res, k_z,
    gain_own, gain_e, gain_x, gain_z, fin, fin_late, rs, rp, rq,
    fsem, usem, csend, crecv, c2send, c2recv, dsend, drecv, msend, mrecv, ksend, krecv, qsend, qrecv, psend, precv,
    xs, xr, zs, zr, g0s, g0r, g1s, g1r, g2s, g2r, h0s, h0r, h1s, h1r, es, er, lqs, lqr, lks, lkr, gs, gr,
    fsend, frecv,
):
    place = where_am_i()
    dp, ep, ctx = place
    torus = Torus(place)
    nall = back
    sources = dict(
        back=(back_hbm, back), nf=(nf_hbm.at[ep], nf), res=(res_hbm, res), og=(og_hbm, og), q=(q_hbm, q_ref),
        kv=(kv_hbm, kv), attT=(attT_hbm, attT), wp=(wp_hbm.at[pl.ds(pl.multiple_of(ep * 128, 128), 128)], wp), y=(y_hbm, y_part),
        nall=(nall_hbm, nall), wq=(wq_hbm, wq), wk=(wk_hbm, wk), wv=(wv_hbm, wv),
    )
    loads = {
        name: pltpu.make_async_copy(src, dst, fsem.at[i]) for i, (name, (src, dst)) in enumerate(sources.items())
    }
    units = {u: pltpu.make_async_copy(gw_hbm.at[u - KEPT], own.at[i], usem.at[i]) for i, u in enumerate(X_UNITS + Z_UNITS)}
    loads["back"].start()
    for u in (3, 10, 4, 11, 5, 6, 7, 8, 9):
        units[u].start()
    for name in ("nf", "res", "og", "kv", "q", "attT", "wp"):
        loads[name].start()
    for name in ("y", "wq", "wk", "wv"):
        loads[name].start()

    def send_to(g, h):
        return (dp, 2 * ctx + g // 2, 2 * (g % 2) + h), (ep, 2 * ctx + g // 2, 2 * (g % 2) + h)

    def is_me(device):
        return (device[0] == dp) & (device[1] == ep) & (device[2] == ctx)

    barrier = pltpu.get_barrier_semaphore()

    def greet_peers(r):
        greet(barrier, (dp, (ep + r) % 8, ctx))
        greet(barrier, torus.at_z(torus.z + r))

    repeat(1, 8, greet_peers)
    repeat(1, 4, lambda r: greet(barrier, torus.at_x(torus.x + r)))

    def greet_senders(i):
        for device in ((dp, i, ep // 2), (i, dp, ep // 2)):

            @pl.when(jnp.logical_not(is_me(device)))
            def _():
                greet(barrier, device)

    repeat(0, 8, greet_senders)
    waits = 17
    for g in range(4):
        for h in range(2):
            for device in send_to(g, h):
                waits = waits + jnp.where(is_me(device), 0, 1)
    pl.semaphore_wait(barrier, waits)

    xa, za = unit_arcs(torus, own, X_UNITS, Z_UNITS, x_slots, z_slots, xs, xr, zs, zr)
    g0 = torus.z_arc(lambda t: rx0.at[t], first_or_last((1, 1)), g0_slots, g0s, g0r)
    g1 = torus.z_arc(lambda t: rx1.at[t], first_or_last((2, 2)), g1_slots, g1s, g1r)
    g2 = torus.z_arc(lambda t: rx2.at[t], first_or_last((1, 2)), g2_slots, g2s, g2r)
    h0 = torus.x_arc(lambda t: rz0.at[t], first_or_last((1, 1)), h0_slots, h0s, h0r)
    h1 = torus.x_arc(lambda t: rz1.at[t], first_or_last((1, 1)), h1_slots, h1s, h1r)

    def finish_x(i):
        target = rx1 if i < 4 else rx2

        def put(index, value):
            target[index[0] * 4 + index[1], i % 4] = value.astype(BF16)

        xa[i].finish(put)

    def finish_z(i):
        def put(index, value):
            rz1[index[0], i] = value.astype(BF16)

        za[i].finish(put)

    total = EpScatterSum(back, cbuf, fbuf, gbuf, csend, crecv, place)
    loads["back"].wait()
    total.start()
    exchange(dg_ref, dbuf, dsend, drecv, place, False)
    dbuf[ep] = dg_ref[ep]
    h0.start()
    for i in range(4):
        units[X_UNITS[i]].wait()
        xa[i].start()
        if i < 2:
            units[Z_UNITS[i]].wait()
            za[i].start()
    g0.start()
    total.far()
    za[0].advance(2)
    xa[0].advance(2)
    za[1].advance(2)
    total.near()
    h0.advance(2)
    xa[1].advance(2)
    g0.advance(2)
    exchange(dg_ref, dbuf, dsend, drecv, place, True)
    for name in ("nf", "res", "og"):
        loads[name].wait()
    gates = gates_ref[...]
    grad_gates = jnp.concatenate([dbuf[p] for p in range(8)], axis=0)
    grad_logits = gates * (grad_gates - jnp.sum(gates * grad_gates, axis=0, keepdims=True))
    high = grad_logits.astype(BF16)
    low = (grad_logits - high.astype(F32)).astype(BF16)
    from_router = mm(high, wr_ref[...], TN) + mm(low, wr_ref[...], TN)
    resid = res[...]
    scale = lax.rsqrt(jnp.mean(resid * resid, axis=-1, keepdims=True) + EPSILON)
    scaled = resid * scale
    za[0].advance(3)
    xa[2].advance(2)
    za[1].advance(3)
    grad_normed = total.last() + from_router
    gain_two = jnp.sum(grad_normed * scaled, axis=0, keepdims=True)
    grad_normed = grad_normed * gain_two_ref[...]
    mean = jnp.mean(grad_normed * scaled, axis=-1, keepdims=True)
    grad_res = og[...].astype(F32) + scale * (grad_normed - scaled * mean)
    gm[ep] = grad_res.astype(BF16)
    gather = EpGather(gm, msend, mrecv, place)
    gather.go(0, 1, 3, 2, 4)
    gres[...] = grad_res
    for t in range(8):
        gain_own[0, 8 + t : 9 + t, :] = gain_two[:, 128 * t : 128 * t + 128]
    xa[3].advance(2)
    g0.advance(3)

    for name in ("kv", "q"):
        loads[name].wait()
    for chunk in range(4):
        part = kv[chunk * CHUNK : (chunk + 1) * CHUNK, :].astype(F32).T
        kT[:, chunk * CHUNK : (chunk + 1) * CHUNK] = part[:HD].astype(BF16)
    gather.got(1)
    gather.go(5, 6)
    gather.got(3)
    gather.go(7, 8)
    za[0].advance(4)
    for chunk in range(4, 8):
        part = kv[chunk * CHUNK : (chunk + 1) * CHUNK, :].astype(F32).T
        kT[:, chunk * CHUNK : (chunk + 1) * CHUNK] = part[:HD].astype(BF16)
    gather.got(2)
    gather.go(9)
    gather.got(4)
    gather.go(10)
    za[1].advance(4)
    repeat(0, 8, lambda j: prepare_queries(j, ctx, start_ref, q_ref, lse_ref, both, stack, rows))
    gather.got(5)
    gather.go(11)
    gather.got(7)
    gather.go(12)
    g0.advance(4)
    to = lax.broadcasted_iota(jnp.int32, (32, 64), 0)
    source = lax.broadcasted_iota(jnp.int32, (32, 64), 1)
    squeeze = jnp.where(source == (to // 4) * 8 + to % 4, 1.0, 0.0).astype(BF16)
    grad_router = mm(mm(squeeze, high).astype(BF16), nf[...]) + mm(mm(squeeze, low).astype(BF16), nf[...])
    side = jnp.concatenate([grad_router, jnp.zeros((96, 1024), F32)], axis=0)
    for d in range(8):
        tile = side[:, d * 128 : (d + 1) * 128].T.astype(BF16)
        for c in range(4):
            early[d // 4, d % 4, c, :, 128:256] = tile[32 * c : 32 * c + 32]
    for i in (4, 5, 6):
        units[X_UNITS[i]].wait()
        xa[i].start()
    for name in ("attT", "wp"):
        loads[name].wait()
    gather.got(0, 6, 8, 9, 10, 11, 12)

    total.sent()
    loads["nall"].start()
    results = EpScatterSum(y_part, cbuf2, fbuf2, gbuf2, c2send, c2recv, place)
    loads["y"].wait()
    results.start()
    repeat(0, 8, lambda j: prepare_grads(j, attT, gm, wp, both, stack, rows))
    grad_proj = mm(attT[0].astype(BF16), gm[0])
    for j in range(1, 8):
        grad_proj = grad_proj + mm(attT[j].astype(BF16), gm[j])
    grad_proj = grad_proj.astype(BF16)
    for d in range(8):
        for c in range(4):
            early[d // 4, d % 4, c, :, 0:128] = grad_proj[32 * c : 32 * c + 32, 128 * d : 128 * d + 128]
    sums_early = Direct(torus, early, e_x, e_res, e_z, es, er)
    sums_q = Direct(torus, late_q, q_x, q_res, q_z, lqs, lqr)
    sums_k = Direct(torus, late_k, k_x, k_res, k_z, lks, lkr)
    sums_early.start()

    lane = lax.broadcasted_iota(jnp.int32, (TOK, 128), 1)

    def chunk_copy(r, m):
        shard = (ctx + r) % 4
        return remote(dkv.at[m, shard], kbuf.at[m, ctx], ksend.at[m, r], krecv.at[m, r], (dp, ep, shard))

    def chunk_go(m):
        for r in (2, 1, 3):
            chunk_copy(r, m).start()
        kbuf[m, ctx] = dkv[m, ctx]

    def piece_copy(src, dst, send, recv, m):
        return remote(src.at[m], dst.at[ep], send.at[m], recv.at[ep], (dp, m, ctx))

    def piece_go(src, dst, send, recv, m):
        @pl.when(ep != m)
        def _():
            piece_copy(src, dst, send, recv, m).start()

        @pl.when(ep == m)
        def _():
            dst[ep] = src[m]

    def pieces_got(src, dst, send, recv):
        def one(r):
            p = (ep + r) % 8
            remote(src.at[p], dst.at[p], send.at[p], recv.at[p], (dp, p, ctx)).wait_recv()

        repeat(1, 8, one)

    def pieces_sent(src, dst, send, recv):
        repeat(1, 8, lambda r: piece_copy(src, dst, send, recv, (ep + r) % 8).wait_send())

    def chunk_done(m):
        for r in (1, 2, 3):
            v = kbuf.at[m, (ctx + 4 - r) % 4]
            remote(v, v, ksend.at[m, r], krecv.at[m, r], (dp, ep, (ctx + r) % 4)).wait_recv()
        grad = kbuf[m, 0].astype(F32) + kbuf[m, 1].astype(F32) + kbuf[m, 2].astype(F32) + kbuf[m, 3].astype(F32)
        cosine, sine = rope_block(4 * m + ctx, ca_ref, sa_ref, cb_ref, sb_ref)
        cosine = jnp.where(lane < HD, cosine, 1.0)
        sine = jnp.where(lane < HD, sine, 0.0)
        dkvb[m] = (grad * cosine - rotate_half(grad) * sine).astype(BF16)
        piece_go(dkvb, kpieces, psend, precv, m)

    def progress(m):
        @pl.when(m == 0)
        def _():
            finish_x(0)
            finish_z(0)
            results.far()

        @pl.when(m == 1)
        def _():
            finish_x(1)
            finish_z(1)
            results.near()

        @pl.when(m == 2)
        def _():
            finish_x(2)
            xa[4].advance(2)
            h1.start()

        @pl.when(m == 3)
        def _():
            finish_x(3)
            g1.start()
            xa[5].advance(2)
            sums_early.turn()

        @pl.when(m == 4)
        def _():
            h1.advance(2)
            xa[6].advance(2)
            out_ref[...] = (res[...] + results.last()).astype(BF16)

        @pl.when(m == 6)
        def _():
            g1.advance(2)

    dqs[...] = jnp.zeros((8, HD, 256), F32)

    def key_chunk(m):
        acc[...] = jnp.zeros((CHUNK, 128), F32)

        def pair(j):
            both_grads, query_grad = attend_pair(m, j, kv, kT, both, stack, rows)
            acc[...] += both_grads
            dqs[j] += query_grad

        repeat(m, 8, pair)
        dkv[m] = acc[...].astype(BF16).reshape(4, TOK, 128)
        chunk_go(m)
        dq = dqs[m] * (HD**-0.5)
        dq = jnp.concatenate([dq[:, :128], dq[:, 128:]], axis=0).T
        cosine, sine = rope_block(4 * m + ctx, ca_ref, sa_ref, cb_ref, sb_ref)
        dqb[m] = (dq * cosine - rotate_half(dq) * sine).astype(BF16)
        piece_go(dqb, qpieces, qsend, qrecv, m)

        @pl.when(m >= 2)
        def _():
            chunk_done(m - 2)

        progress(m)

    repeat(0, 8, key_chunk)
    chunk_done(6)
    for name in ("nall", "wq"):
        loads[name].wait()

    def weights(grad, late):
        out = mm(nall[...].reshape(1024, 1024), grad.reshape(1024, 128), TN).astype(BF16)
        for d in range(8):
            for c in range(4):
                at = d * 128 + c * 32
                late[d // 4, d % 4, c] = out[at : at + 32]

    weights(dqb[...], late_q)
    sums_q.start()
    chunk_done(7)
    weights(dkvb[...], late_k)
    sums_k.start()
    pieces_got(dqb, qpieces, qsend, qrecv)
    grad_q = jnp.concatenate([qpieces[p] for p in range(8)], axis=1)
    grad_normed = mm(grad_q, wq[...], NT)

    def piece(g, h, kind, device):
        index = (kind * 4 + g) * 2 + h
        src = (fin.at[g, :, pl.ds(128, 128)], fin.at[g, :, pl.ds(0, 128)], fin_late.at[g])[kind]
        mine = dp if kind == 1 else ep
        return remote(src, (rs, rp, rq)[kind].at[mine], fsend.at[index], frecv.at[kind, mine], device)

    def each_piece(kinds, act, local):
        def one(i):
            g, h = i // 2, i % 2
            for kind in kinds:
                device = send_to(g, h)[kind % 2]

                @pl.when(jnp.logical_not(is_me(device)))
                def _():
                    act(piece(g, h, kind, device))

                if local:

                    @pl.when(is_me(device))
                    def _():
                        if kind == 0:
                            rs[ep] = fin[g, :, 128:256]
                        elif kind == 1:
                            rp[dp] = fin[g, :, 0:128]
                        else:
                            rq[ep] = fin_late[g]

        repeat(0, 8, one)

    def pieces_in(kind):
        def one(i):
            device = (i, dp, ep // 2) if kind == 1 else (dp, i, ep // 2)

            @pl.when(jnp.logical_not(is_me(device)))
            def _():
                dst = (rs, rp, rq)[kind].at[i]
                remote(dst, dst, fsend.at[kind * 8], frecv.at[kind, i], device).wait_recv()

        repeat(0, 8, one)

    done_early = sums_early.finish()
    for g in range(4):
        fin[g] = done_early[8 * g : 8 * g + 8]
    each_piece((0, 1), lambda c: c.start(), True)
    g1.advance(3)
    for name in ("wk", "wv"):
        loads[name].wait()
    pieces_got(dkvb, kpieces, psend, precv)
    grad_k = jnp.concatenate([kpieces[p, :, 0:HD] for p in range(8)], axis=1)
    grad_v = jnp.concatenate([kpieces[p, :, HD:128] for p in range(8)], axis=1)
    grad_normed = grad_normed + mm(grad_k, wk[...], NT) + mm(grad_v, wv[...], NT)
    x = x_ref[...].astype(F32)
    scale = lax.rsqrt(jnp.mean(x * x, axis=-1, keepdims=True) + EPSILON)
    scaled = x * scale
    gain_one = jnp.sum(grad_normed * scaled, axis=0, keepdims=True)
    for t in range(8):
        gain_own[0, t : t + 1, :] = gain_one[:, 128 * t : 128 * t + 128]

    def gain_copy(stage, r):
        src = gain_own.at[stage]
        if stage == 0:
            dst, device, base = gain_e.at[r - 1], (dp, (ep + r) % 8, ctx), 0
        elif stage == 1:
            dst, device, base = gain_x.at[r - 1], torus.at_x(torus.x + r), 7
        else:
            dst, device, base = gain_z.at[r - 1], torus.at_z(torus.z + r), 10
        return remote(src, dst, gs.at[base + r], gr.at[base + r], device)

    def gain_stage(stage, count):
        if stage > 0:
            last, slots = ((7, gain_e), (3, gain_x), (7, gain_z))[stage - 1]
            repeat(1, last + 1, lambda r: gain_copy(stage - 1, r).wait_recv())
            value = gain_own[stage - 1]
            for r in range(1, last + 1):
                value = value + slots[r - 1]
            gain_own[stage] = value
        repeat(1, count + 1, lambda r: gain_copy(stage, r).start())

    gain_stage(0, 7)
    grad_normed = grad_normed * gain_one_ref[...]
    mean = jnp.mean(grad_normed * scaled, axis=-1, keepdims=True)
    ing_ref[...] = (gres[...] + scale * (grad_normed - scaled * mean)).astype(BF16)

    sums_q.turn()
    gain_stage(1, 3)
    sums_k.turn()
    for i in (4, 5, 6):
        finish_x(i)
    g2.start()
    gain_stage(2, 7)

    done_q, done_k = sums_q.finish(), sums_k.finish()
    for g in range(4):
        at = slice(8 * g, 8 * g + 8)
        fin_late[g, :, 0:128] = done_q[at]
        fin_late[g, :, 128:256] = done_k[at]
    each_piece((2,), lambda c: c.start(), True)

    g1.advance(4)
    g2.advance(2)

    def put_unit(unit, value):
        j, u = unit // 3, unit % 3
        if u < 2:
            gin_ref[j, 16 * u : 16 * u + 16, :] = value
        else:
            gout_ref[j] = value

    def finish_units(arc, units):
        for way in (0, 1):
            arc.copy(way, arc.steps).wait_recv()
        mine = arc.own(arc.pos)
        up, down = arc.slots.at[0, arc.steps - 1], arc.slots.at[1, arc.steps - 1]
        for i, unit in enumerate(units):
            put_unit(unit, mine[i].astype(F32) + up[i].astype(F32) + down[i].astype(F32))

    for way in (0, 1):
        h0.copy(way, 2).wait_recv()
    for h in (0, 1):
        value = rz0[torus.x, h].astype(F32) + h0_slots[0, 1, h].astype(F32) + h0_slots[1, 1, h].astype(F32)
        gout_ref[0, :, 512 * h : 512 * h + 512] = value
    finish_units(h1, Z_UNITS)
    finish_units(g0, X_FIRST)
    g2.advance(3)
    finish_units(g1, X_UNITS[:4])
    pieces_in(0)
    pieces_in(1)
    last = gain_own[2]
    repeat(1, 8, lambda r: gain_copy(2, r).wait_recv())
    for r in range(7):
        last = last + gain_z[r]
    gain_own[3] = last

    g2.advance(4)
    pieces_in(2)
    odd = ctx % 2 == 1

    def mine(v):
        return jnp.where(odd, v[4:8], v[0:4])

    gq_ref[...] = mine(jnp.concatenate([rq[i, :, 0:128] for i in range(8)], axis=1))
    gk_ref[...] = mine(jnp.concatenate([rq[i, :, 128:192] for i in range(8)], axis=1))
    gv_ref[...] = mine(jnp.concatenate([rq[i, :, 192:256] for i in range(8)], axis=1))
    side = rs[0]
    for i in range(1, 8):
        side = side + rs[i]
    gside_ref[...] = mine(side)
    gproj_out[...] = mine(jnp.concatenate([rp[i] for i in range(8)], axis=1))
    for which in (0, 1):
        row = jnp.broadcast_to(gain_own[3, pl.ds(8 * which + dp, 1), :], (8, 128))
        gains_ref[8 * which : 8 * which + 8, :] = pltpu.roll(row, (128 - 16 * ep - 4 * ctx) % 128, 1)

    finish_units(g2, X_UNITS[4:])

    results.sent()
    gather.sent()
    exchange_sent(dg_ref, dbuf, dsend, drecv, place)
    pieces_sent(dqb, qpieces, qsend, qrecv)
    pieces_sent(dkvb, kpieces, psend, precv)

    def chunk_sent(m):
        for r in (1, 2, 3):
            chunk_copy(r, m).wait_send()

    repeat(0, 8, chunk_sent)
    for arc in xa + za + [g0, g1, g2, h0, h1]:
        arc.sent()
    for sums in (sums_early, sums_q, sums_k):
        sums.sent()
    for stage, count in ((0, 7), (1, 3), (2, 7)):
        repeat(1, count + 1, lambda r: gain_copy(stage, r).wait_send())
    each_piece((0, 1, 2), lambda c: c.wait_send(), False)


def pack_kernel(*refs):
    count = len(refs) // 2
    for src, dst in zip(refs[:count], refs[count:]):
        dst[...] = src[...]


def call(kernel, outs, scratch, args, name, collective=None, **more):
    params = dict(vmem_limit_bytes=VMEM_LIMIT)
    if collective is not None:
        params.update(collective_id=collective, has_side_effects=True)
    space = pl.BlockSpec(memory_space=pltpu.VMEM)
    return pl.pallas_call(
        kernel,
        out_shape=[jax.ShapeDtypeStruct(shape, kind) for shape, kind in outs],
        in_specs=more.pop("in_specs", [space] * len(args)),
        out_specs=more.pop("out_specs", [space] * len(outs)),
        scratch_shapes=scratch,
        compiler_params=pltpu.CompilerParams(**params),
        name=name,
        **more,
    )(*args)


def sems(*sizes):
    return [pltpu.SemaphoreType.DMA(s if isinstance(s, tuple) else (s,)) for s in sizes]


def body(
    layer_input, gain_attn, w_query, w_key, w_value, w_proj, gain_ffn, w_router,
    w_expert_in, w_expert_out, segment_ids, expert_ids, slot_order, out_grad,
):
    ep = lax.axis_index("ep")
    gain_one, gain_two = gain_attn.reshape(1, 1024), gain_ffn.reshape(1, 1024)
    tables = [jnp.asarray(t) for t in rope_tables()]
    w_own = jnp.concatenate(
        [
            lax.dynamic_slice_in_dim(w_query, ep * 128, 128, 1),
            lax.dynamic_slice_in_dim(w_key, ep * 64, 64, 1),
            lax.dynamic_slice_in_dim(w_value, ep * 64, 64, 1),
        ],
        axis=1,
    )
    wr_rows = jnp.pad(w_router.T.reshape(8, 4, 1024), ((0, 0), (0, 4), (0, 0))).reshape(64, 1024)
    order = slot_order.reshape(TOK, 8)
    docs = segment_ids.reshape(32, 128)

    normed_all, query, kv, grad_all, slots, chosen, starts = call(
        first_kernel,
        [
            ((8, TOK, 1024), BF16), ((8, TOK, 128), BF16), ((8, 4, TOK, 128), BF16), ((8, TOK, 1024), BF16),
            ((8, 8, TOK), F32), ((64, TOK), F32), ((32, 128), F32),
        ],
        [pltpu.VMEM((8, 8, TOK), F32)] + sems(13, 13, 13, 13, 8, 8, 24, 24),
        [layer_input, gain_one, out_grad, w_own, *tables, expert_ids, expert_ids.T, order, order.T, docs],
        "first", 1,
    )
    kv_rows = kv.reshape(4096, 128)
    ctx = lax.axis_index("ctx")
    first = lax.dynamic_slice_in_dim(starts.reshape(8, 4, 128), ctx, 1, 1)[:, 0, 0].astype(jnp.int32) // CHUNK

    vm, sm = pl.BlockSpec(memory_space=pltpu.VMEM), pl.BlockSpec(memory_space=pltpu.SMEM)
    attended, attended_tall, log_sums = call(
        attend_kernel,
        [((8, TOK, 128), BF16), ((8, 128, TOK), F32), ((8, 8, 256), F32)],
        [pltpu.VMEM((128, 4096), BF16)],
        [first, query, kv_rows, starts],
        "attend", in_specs=[sm, vm, vm, vm],
    )
    residual, ffn_all, gates_in, gates = call(
        middle_kernel,
        [((TOK, 1024), F32), ((8, TOK, 1024), BF16), ((8, 8, TOK), F32), ((64, TOK), F32)],
        [pltpu.VMEM((8, TOK, 128), BF16), pltpu.VMEM((8, 8, TOK), F32)] + sems(8, 8, 13, 13, 8, 8),
        [attended, layer_input, gain_two, w_proj, wr_rows, chosen],
        "middle", 2,
    )
    hbm = pl.BlockSpec(memory_space=pl.ANY)
    wide = pltpu.VMEM((8, TOK, 1024), BF16)
    ex, ez = len(X_FIRST), len(Z_FIRST)
    sums, back, grad_gates, sums_x, sums_z, units = call(
        expert_kernel,
        [
            ((8, TOK, 1024), BF16), ((8, TOK, 1024), BF16), ((8, 8, TOK), F32), ((8, ex, 16, 1024), BF16),
            ((4, 2, 16, 512), BF16), ((12 - KEPT, 2, 4, 4, 16, 1024), BF16),
        ],
        [
            wide, wide, pltpu.VMEM((2, 1024, 1024), BF16), pltpu.VMEM((2, 512, 1024), BF16),
            pltpu.VMEM((4, 8 * CAP, 1024), F32), pltpu.VMEM((4, 8 * CAP, 1024), F32),
            pltpu.VMEM((12, 2, 4, 4, 16, 1024), BF16),
            pltpu.VMEM((ex, 2, 2, 2, 4, 16, 1024), BF16), pltpu.VMEM((ez, 2, 4, 4, 16, 1024), BF16),
        ]
        + sems(2, (4, 2), 12 - KEPT, (ex, 2, 2), (ex, 2, 2), (ez, 2, 4), (ez, 2, 4)),
        [slots, gates_in, ffn_all, grad_all, w_expert_in, w_expert_out],
        "experts", 4, in_specs=[vm, vm] + [hbm] * 4, out_specs=[vm] * 5 + [hbm],
    )
    nx, nz = len(X_UNITS), len(Z_UNITS)
    block = pltpu.VMEM((8, TOK, 128), BF16)

    def direct(lanes):
        return [
            pltpu.VMEM((3, 2, 4, 32, lanes), BF16), pltpu.VMEM((8, 32, lanes), BF16), pltpu.VMEM((7, 32, lanes), BF16)
        ]

    results = call(
        tail_kernel,
        [
            ((TOK, 1024), BF16), ((TOK, 1024), BF16), ((4, 32, 1024), F32), ((4, 16, 1024), F32), ((4, 1024), F32),
            ((4, 512), F32), ((4, 512), F32), ((4, 128), F32), ((4, 1024), F32), ((16, 128), F32),
        ],
        [
            wide, pltpu.VMEM((TOK, 1024), BF16), pltpu.VMEM((TOK, 1024), F32), pltpu.VMEM((TOK, 1024), BF16), block,
            pltpu.VMEM((4096, 128), BF16), pltpu.VMEM((8, 128, TOK), F32), pltpu.VMEM((128, 1024), BF16), wide,
            pltpu.VMEM((1024, 1024), BF16), pltpu.VMEM((1024, 512), BF16), pltpu.VMEM((1024, 512), BF16),
            pltpu.VMEM((nx + nz, 2, 4, 4, 16, 1024), BF16),
            pltpu.VMEM((8, 8, TOK), F32),
        ]
        + scatter_sum_scratch()[:3] * 2
        + [
            wide, pltpu.VMEM((TOK, 1024), F32),
            pltpu.VMEM((HD, 4096), BF16), pltpu.VMEM((8, 128, 512), BF16), pltpu.VMEM((8, 512, 128), BF16),
            pltpu.VMEM((8, 8, 256), F32), pltpu.VMEM((8, HD, 256), F32), pltpu.VMEM((CHUNK, 128), F32),
            pltpu.VMEM((8, 4, TOK, 128), BF16),
            block, block, pltpu.VMEM((8, 4, TOK, 128), BF16), block, block,
            pltpu.VMEM((nx, 2, 2, 2, 4, 16, 1024), BF16), pltpu.VMEM((nz, 2, 4, 4, 16, 1024), BF16),
            pltpu.VMEM((2, 4, ex, 16, 1024), BF16), pltpu.VMEM((2, 4, 4, 16, 1024), BF16), pltpu.VMEM((2, 4, 3, 16, 1024), BF16),
            pltpu.VMEM((2, 2, 2, 16, 512), BF16), pltpu.VMEM((2, 2, nz, 16, 1024), BF16),
            pltpu.VMEM((8, 4, 16, 1024), BF16), pltpu.VMEM((8, 3, 16, 1024), BF16), pltpu.VMEM((4, nz, 16, 1024), BF16),
            pltpu.VMEM((2, 4, 4, 32, 256), BF16), pltpu.VMEM((2, 4, 4, 32, 128), BF16), pltpu.VMEM((2, 4, 4, 32, 128), BF16),
        ]
        + direct(256) + direct(128) + direct(128)
        + [
            pltpu.VMEM((4, 16, 128), F32), pltpu.VMEM((7, 16, 128), F32), pltpu.VMEM((3, 16, 128), F32),
            pltpu.VMEM((7, 16, 128), F32),
            pltpu.VMEM((4, 8, 256), F32), pltpu.VMEM((4, 8, 256), F32), pltpu.VMEM((8, 8, 128), F32),
            pltpu.VMEM((8, 8, 128), F32), pltpu.VMEM((8, 8, 256), F32),
        ]
        + sems(
            13, nx + nz, 8, 8, 8, 8, 8, 8, 13, 13, (8, 4), (8, 4), 8, 8, 8, 8,
            (nx, 2, 2), (nx, 2, 2), (nz, 2, 4), (nz, 2, 4),
            (2, 4), (2, 4), (2, 4), (2, 4), (2, 4), (2, 4), (2, 2), (2, 2), (2, 2), (2, 2), 11, 11, 11, 11, 11, 11, 18, 18,
            24, (3, 8),
        ),
        [
            grad_gates, gates, gain_two, wr_rows, layer_input, gain_one, *tables, starts, log_sums,
            sums_x, sums_z, back, ffn_all, residual, out_grad, query, kv_rows, attended_tall, w_proj, sums, normed_all,
            w_query, w_key, w_value, units,
        ],
        "tail", 3, in_specs=[vm] * 14 + [hbm] * 14,
    )
    layer_output, input_grad, grad_in, grad_out, out_q, out_k, out_v, side, out_proj, gains = call(
        pack_kernel, [(r.shape, r.dtype) for r in results], [], results, "pack"
    )
    return (
        layer_output, input_grad, gains[0, :4], out_q, out_k, out_v, out_proj, gains[8, :4], side[:, :32], grad_in, grad_out,
    )


def solution(mesh):
    tokens = P(("dp", "ep", "ctx"), None)
    in_specs = (
        tokens, P(), P(), P(), P(), P(), P(), P(),
        P("ep", None, None), P("ep", None, None), P("dp", None), tokens, tokens, tokens,
    )
    out_specs = (
        tokens, tokens, P(("dp", "ep", "ctx")), tokens, tokens, tokens, tokens, P(("dp", "ep", "ctx")), tokens,
        P("ep", ("dp", "ctx"), None), P("ep", ("dp", "ctx"), None),
    )
    return jax.shard_map(body, mesh=mesh, in_specs=in_specs, out_specs=out_specs, check_vma=False)
```

profile of v0, /device:TPU:8, one launch (start us, length us, event | category | flops | bytes accessed | tf_op | source)
XLA Modules:
  0.0 249.9 jit_solution(12854273156016222635)
XLA Ops:
  0.6 0.5 broadcast.18
  1.2 1.3 reduce.3
  2.5 0.1 reshape.48.so_ref
  2.6 0.0 copy-start
  2.6 0.7 copy.32
  3.3 0.9 reshape.53
  4.1 0.7 pad_bitcast_fusion.wr_ref
  4.8 1.4 copy.33.eid_ref
  6.2 1.0 constant_dynamic-slice_fusion.3
  7.2 1.3 constant_dynamic-slice_fusion.1
  8.5 1.0 pad_maximum_fusion.w_ref
  9.4 0.0 copy-done
  9.4 37.2 %first.1 = (bf16[8,128,1024]{2,1,0:T(8,128)(2,1)}, bf16[8,128,128]{2,1,0:T(8,128)(2,1)}, bf16[8,4,128,128]{3,2,1,0:T(8,128)(2,1)}, bf16[8,128,1024]{2,1,0:T(8,12...) custom-call(bf16[128,1024]{1,0:T(8,128)(2,1)} %x_ref.5, f32[1,1024]{1,0:T(1,128)} %bitcast.28, ...), custom_call_target="tpu_custom_call" | custom-call | tf_op jit(solution)/shard_map/first/pallas_call | solution.py:1397
  46.6 0.7 constant_dynamic-slice_fusion
  47.3 0.1 copy.36
  47.4 0.5 and_select_fusion.first_ref
  47.9 19.0 %attend.1 = (bf16[8,128,128]{2,1,0:T(8,128)(2,1)}, f32[8,128,128]{2,1,0:T(8,128)}, f32[8,8,256]{2,1,0:T(8,128)}) custom-call(s32[8]{0:T(128)} %and_select_fusion.first_ref, bf16[8,128,128]{2,1,0:T(8,128)(2,1)} %get-tuple-element.53.q_ref.q_hbm, bf16[4096,128]{1,0:T(8,128)(2,1)} %bitcast.23, f32[32,128]{1,0:T(8,128)} %get-tuple-element.52.start_ref), custom_call_target="tpu_custom_call" | custom-call | tf_op jit(solution)/shard_map/attend/pallas_call | solution.py:1397
  66.9 25.7 %middle.1 = (f32[128,1024]{1,0:T(8,128)}, bf16[8,128,1024]{2,1,0:T(8,128)(2,1)}, f32[8,8,128]{2,1,0:T(8,128)}, f32[64,128]{1,0:T(8,128)}) custom-call(bf16[8,128,128]{2,1,0:T(8,128)(2,1)} %get-tuple-element.55.att_ref, bf16[128,1024]{1,0:T(8,128)(2,1)} %x_ref.5, f32[1,1024]{1,0:T(1,128)} %bitcast.30, bf16[1024,1024]{1,0:T(8,128)(2,1)} %wp_hbm.1, ...), custom_call_target="tpu_custom_call" | custom-call | tf_op jit(solution)/shard_map/middle/pallas_call | solution.py:1397
  92.6 36.6 %experts.1 = (bf16[8,128,1024]{2,1,0:T(8,128)(2,1)}, bf16[8,128,1024]{2,1,0:T(8,128)(2,1)}, f32[8,8,128]{2,1,0:T(8,128)}, bf16[8,2,16,1024]{3,2,1,0:T(8,128)(2,1...) custom-call(f32[8,8,128]{2,1,0:T(8,128)} %get-tuple-element.51.slot_ref, ...), custom_call_target="tpu_custom_call" | custom-call | tf_op jit(solution)/shard_map/experts/pallas_call | solution.py:1397
  129.3 117.0 %tail.1 = (bf16[128,1024]{1,0:T(8,128)(2,1)}, bf16[128,1024]{1,0:T(8,128)(2,1)}, f32[4,32,1024]{2,1,0:T(8,128)}, f32[4,16,1024]{2,1,0:T(8,128)}, f32[4,1024]{1,0...) custom-call(f32[8,8,128]{2,1,0:T(8,128)} %get-tuple-element.60.dg_re, ...), custom_call_target="tpu_custom_call" | custom-call | tf_op jit(solution)/shard_map/tail/pallas_call | solution.py:1397
  246.2 2.5 pack.1
  248.7 1.2 slice_bitcast_fusion
Async XLA Ops:
  2.6 6.8 %copy-start = (s32[128,8]{1,0:T(8,128)}, s32[128,8]{1,0:T(8,128)S(1)}, u32[]{:S(2)}) copy-start(s32[128,8]{1,0:T(8,128)S(1)} %reshape.48.so_ref) | copy-start | bytes 12292
where the time goes:
time: 250 us
  Pallas kernels  238 us (95%)
  local copies, waits for them, and re-layouts  8.46 us (3%)
  other arithmetic  2.83 us (1%)
    pallas_call x6, Pallas kernels, call(): pl.pallas_call(kernel, out_shape=[jax.ShapeDtypeStruct(shape, kind) for s...  238 us

commit v1 on v0

--- a/solution.py
+++ b/solution.py
@@ -261,17 +261,15 @@
     return jnp.maximum(value, above)
 
 
-def slots_of(eid_ref, eidT_ref, so_ref, soT_ref, slot_scr, sel_ref):
+def slots_of(eidT_ref, soT_ref, slot_scr, sel_ref):
     def expert(index):
         return jnp.where(index % 8 < 4, (index // 8) * 4 + index % 8, -1)
 
     row_expert = expert(lax.broadcasted_iota(jnp.int32, (64, TOK), 0))
-    lane_expert = expert(lax.broadcasted_iota(jnp.int32, (TOK, 64), 1))
     by_row = jnp.full((64, TOK), BIG, F32)
-    by_lane = jnp.full((TOK, 64), BIG, F32)
     for k in range(8):
         by_row = jnp.where(eidT_ref[k : k + 1, :] == row_expert, soT_ref[k : k + 1, :].astype(F32), by_row)
-        by_lane = jnp.where(eid_ref[:, k : k + 1] == lane_expert, so_ref[:, k : k + 1].astype(F32), by_lane)
+    by_lane = by_row.T
     sel_ref[...] = jnp.where(by_row < BIG, 1.0, 0.0)
     for g in range(8):
         for j in range(4):
@@ -283,17 +281,55 @@
         slot_scr[g, 4:8, :] = jnp.full((4, TOK), -1.0, F32)
 
 
-def first_kernel(
-    x_ref, gain_ref, og_ref, w_ref, ca_ref, sa_ref, cb_ref, sb_ref, eid_ref, eidT_ref, so_ref, soT_ref, doc_ref,
-    nall_ref, q_ref, kv_ref, ogall_ref, slot_ref, sel_ref, start_ref,
-    slot_scr, nsend, nrecv, osend, orecv, ssend, srecv, ksend, krecv,
+CHUNK = 512
+
+
+def key_mask(chunk, start_row, place_row):
+    keys = (lax.broadcasted_iota(jnp.int32, (CHUNK, 256), 0) + chunk * CHUNK).astype(F32)
+    return (keys >= start_row) & (keys <= place_row)
+
+
+def query_rows(j, ctx, start_ref):
+    block = 4 * j + ctx
+    start = start_ref[pl.ds(block, 1), :]
+    places = (lax.broadcasted_iota(jnp.int32, (1, 128), 1) + block * 128).astype(F32)
+    return jnp.concatenate([start, start], axis=1), jnp.concatenate([places, places], axis=1)
+
+
+def turned(block):
+    return block.astype(F32).T.astype(BF16)
+
+
+def heads_wide(tall):
+    return jnp.concatenate([tall[:HD], tall[HD:]], axis=1)
+
+
+def head_kernel(
+    x_ref, gain_one_ref, gain_two_ref, og_ref, ca_ref, sa_ref, cb_ref, sb_ref, eidT_ref, soT_ref, doc_ref, wr_ref,
+    wq_hbm, wk_hbm, wv_hbm, wp_hbm,
+    nall_ref, ogall_ref, q_ref, kv_ref, slot_ref, start_ref, attT_ref, lse_ref, res_ref, nf_ref, gin_ref, gates_ref,
+    wq, wk, wv, w_own, wp, slot_scr, sel, att, abuf, kv_rows, kvT, gscr,
+    wsem, nsend, nrecv, osend, orecv, ssend, srecv, ksend, krecv, asend, arecv, fsend, frecv, gsend, grecv,
 ):
     place = where_am_i()
     dp, ep, ctx = place
     y = ep // 2
+    pair = pl.ds(pl.multiple_of(y * 128, 128), 128)
+    loads = [
+        pltpu.make_async_copy(src, dst, wsem.at[i])
+        for i, (src, dst) in enumerate(
+            (
+                (wq_hbm.at[:, pl.ds(pl.multiple_of(ep * 128, 128), 128)], wq),
+                (wk_hbm.at[:, pair], wk),
+                (wv_hbm.at[:, pair], wv),
+                (wp_hbm, wp),
+            )
+        )
+    ]
+    for f in loads:
+        f.start()
     barrier = pltpu.get_barrier_semaphore()
-    for r in range(1, 8):
-        greet(barrier, (dp, (ep + r) % 8, ctx))
+    repeat(1, 8, lambda r: greet(barrier, (dp, (ep + r) % 8, ctx)))
 
     @pl.when(ctx > 0)
     def _():
@@ -304,7 +340,7 @@
         greet(barrier, (dp, ep, ctx + 1))
 
     x = x_ref[...].astype(F32)
-    normed = x * lax.rsqrt(jnp.mean(x * x, axis=-1, keepdims=True) + EPSILON) * gain_ref[...]
+    normed = x * lax.rsqrt(jnp.mean(x * x, axis=-1, keepdims=True) + EPSILON) * gain_one_ref[...]
     nall_ref[ep] = normed.astype(BF16)
     ogall_ref[ep] = og_ref[...]
     edges = jnp.where(ctx > 0, 1, 0) + jnp.where(ctx < 3, 1, 0)
@@ -313,18 +349,21 @@
     gather = EpGather(nall_ref, nsend, nrecv, place)
     grads = EpGather(ogall_ref, osend, orecv, place)
     gather.go(0, 1, 3, 2, 4)
-
-    start_ref[...] = starts_of(doc_ref[...])
-    slots_of(eid_ref, eidT_ref, so_ref, soT_ref, slot_scr, sel_ref)
-    slot_ref[ep] = slot_scr[ep]
-    exchange(slot_scr, slot_ref, ssend, srecv, place, False)
-
+    for f in loads[:3]:
+        f.wait()
+    lane = lax.broadcasted_iota(jnp.int32, (1024, 128), 1)
+    even = ep % 2 == 0
+    k_pair, v_pair = wk[...].astype(F32), wv[...].astype(F32)
+    k_half = jnp.where(even, k_pair, pltpu.roll(k_pair, HD, 1))
+    v_half = jnp.where(even, pltpu.roll(v_pair, HD, 1), v_pair)
+    w_own[:, 0:128] = wq[...]
+    w_own[:, 128:256] = jnp.where(lane < HD, k_half, v_half).astype(BF16)
     lane = lax.broadcasted_iota(jnp.int32, (TOK, 128), 1)
 
     def project(dy):
         chip = (y + dy) % 4
         rows = jnp.concatenate([nall_ref[2 * chip], nall_ref[2 * chip + 1]], axis=0)
-        out = mm(rows, w_ref[...])
+        out = mm(rows, w_own[...])
         for i in range(2):
             b = 2 * chip + i
             cosine, sine = rope_block(4 * b + ctx, ca_ref, sa_ref, cb_ref, sb_ref)
@@ -372,6 +411,8 @@
     gather.got(0)
     project(0)
     hops(1, 0)
+    start_ref[...] = starts_of(doc_ref[...])
+    slots_of(eidT_ref, soT_ref, slot_scr, sel)
     gather.got(1)
     gather.go(5, 6)
     gather.got(3)
@@ -380,20 +421,22 @@
     gather.go(9)
     gather.got(4)
     gather.go(10)
-    grads.go(0, 1, 3, 2, 4)
+    slot_ref[ep] = slot_scr[ep]
+    exchange(slot_scr, slot_ref, ssend, srecv, place, False)
+    hops(2, 0)
     gather.got(6, 9)
     project(3)
     hops(1, 1)
-    hops(2, 0)
     gather.got(8, 10)
     project(1)
     hops(1, 2)
+    hops(3, 0)
     hops(2, 1)
-    hops(3, 0)
     gather.got(5)
     gather.go(11)
     gather.got(7)
     gather.go(12)
+    grads.go(0, 1, 3, 2, 4)
     gather.got(11, 12)
     project(2)
     hops(1, 3)
@@ -401,53 +444,29 @@
     hops(3, 1)
     hops(2, 3)
     hops(3, 2)
-    grads.whole()
     hops(3, 3)
+    grads.got(1)
+    grads.go(5, 6)
+    grads.got(3)
+    grads.go(7, 8)
     for g in range(4):
         for direction in (0, 1):
             hop(direction, 3, g, "recv")
-    exchange(slot_scr, slot_ref, ssend, srecv, place, True)
-    gather.sent()
-    grads.sent()
-    exchange_sent(slot_scr, slot_ref, ssend, srecv, place)
-    for g in range(4):
-        for h in (1, 2, 3):
-            for direction in (0, 1):
-                hop(direction, h, g, "sent")
-
-
-CHUNK = 512
-
-
-def key_mask(chunk, start_row, place_row):
-    keys = (lax.broadcasted_iota(jnp.int32, (CHUNK, 256), 0) + chunk * CHUNK).astype(F32)
-    return (keys >= start_row) & (keys <= place_row)
-
-
-def query_rows(j, ctx, start_ref):
-    block = 4 * j + ctx
-    start = start_ref[pl.ds(block, 1), :]
-    places = (lax.broadcasted_iota(jnp.int32, (1, 128), 1) + block * 128).astype(F32)
-    return jnp.concatenate([start, start], axis=1), jnp.concatenate([places, places], axis=1)
-
-
-def turned(block):
-    return block.astype(F32).T.astype(BF16)
-
-
-def heads_wide(tall):
-    return jnp.concatenate([tall[:HD], tall[HD:]], axis=1)
-
-
-def attend_kernel(first_ref, q_ref, kv_ref, start_ref, att_ref, attT_ref, lse_ref, kvT):
-    ctx = lax.axis_index("ctx")
-
-    for chunk in range(8):
-        part = kv_ref[chunk * CHUNK : (chunk + 1) * CHUNK, :].astype(F32).T
+
+    def turn_keys(chunk):
+        rows = kv_ref[chunk].reshape(CHUNK, 128)
+        at = pl.ds(pl.multiple_of(chunk * CHUNK, CHUNK), CHUNK)
+        kv_rows[at, :] = rows
+        part = rows.astype(F32).T
         row = lax.broadcasted_iota(jnp.int32, part.shape, 0)
-        kvT[:, chunk * CHUNK : (chunk + 1) * CHUNK] = jnp.where(row < HD, 1.0, part).astype(BF16)
-
-    for j in range(8):
+        kvT[:, at] = jnp.where(row < HD, 1.0, part).astype(BF16)
+
+    repeat(0, 8, turn_keys)
+
+    def piece_copy(m):
+        return remote(att.at[m], abuf.at[ep], asend.at[m], arecv.at[ep], (dp, m, ctx))
+
+    def block(j):
         start_row, place_row = query_rows(j, ctx, start_ref)
         wide = heads_wide(turned(q_ref[j]))
         q_pad = jnp.concatenate([wide, jnp.zeros_like(wide)], axis=0)
@@ -455,48 +474,57 @@
         def step(chunk, carry):
             top, total = carry
             rows = pl.ds(pl.multiple_of(chunk * CHUNK, CHUNK), CHUNK)
-            scores = mm(kv_ref[rows, :], q_pad)
+            scores = mm(kv_rows[rows, :], q_pad)
             scores = jnp.where(key_mask(chunk, start_row, place_row), scores, MASKED)
             new_top = jnp.maximum(top, jnp.max(scores, axis=0, keepdims=True))
             probs = jnp.exp(scores - new_top).astype(BF16)
             total = total * jnp.exp(top - new_top) + mm(kvT[:, rows], probs)
             return new_top, total
 
-        top, total = lax.fori_loop(
-            first_ref[j], j + 1, step, (jnp.full((1, 256), MASKED, F32), jnp.zeros((128, 256), F32))
-        )
+        top, total = lax.fori_loop(0, j + 1, step, (jnp.full((1, 256), MASKED, F32), jnp.zeros((128, 256), F32)))
         norm = total[0:1]
         out = total[HD:] / norm
         tall = jnp.concatenate([out[:, :128], out[:, 128:]], axis=0)
         attT_ref[j] = tall
-        att_ref[j] = tall.T.astype(BF16)
+        att[j] = tall.T.astype(BF16)
         lse_ref[j] = jnp.broadcast_to(top + jnp.log(norm), (8, 256))
 
-
-def middle_kernel(
-    att_ref, x_ref, gain_ref, w_ref, wr_ref, sel_ref,
-    res_ref, nf_ref, gin_ref, gates_ref,
-    abuf, gscr, asend, arecv, nsend, nrecv, gsend, grecv,
-):
-    place = where_am_i()
-    dp, ep, ctx = place
-    barrier = pltpu.get_barrier_semaphore()
-    for r in range(1, 8):
-        greet(barrier, (dp, (ep + r) % 8, ctx))
-    pl.semaphore_wait(barrier, 7)
-    exchange(att_ref, abuf, asend, arecv, place, False)
-    abuf[ep] = att_ref[ep]
-    exchange(att_ref, abuf, asend, arecv, place, True)
+        @pl.when(ep != j)
+        def _():
+            piece_copy(j).start()
+
+        @pl.when(ep == j)
+        def _():
+            abuf[ep] = att[j]
+
+    repeat(0, 6, block)
+    grads.got(2)
+    grads.go(9)
+    grads.got(4)
+    grads.go(10)
+    grads.got(5)
+    grads.go(11)
+    grads.got(7)
+    grads.go(12)
+    repeat(6, 8, block)
+
+    loads[3].wait()
+
+    def piece_got(r):
+        p = (ep + r) % 8
+        remote(att.at[p], abuf.at[p], asend.at[p], arecv.at[p], (dp, p, ctx)).wait_recv()
+
+    repeat(1, 8, piece_got)
     attended = jnp.concatenate([abuf[p] for p in range(8)], axis=1)
-    res = x_ref[...].astype(F32) + mm(attended, w_ref[...])
+    res = x_ref[...].astype(F32) + mm(attended, wp[...])
     res_ref[...] = res
-    normed = res * lax.rsqrt(jnp.mean(res * res, axis=-1, keepdims=True) + EPSILON) * gain_ref[...]
+    normed = res * lax.rsqrt(jnp.mean(res * res, axis=-1, keepdims=True) + EPSILON) * gain_two_ref[...]
     normed = normed.astype(BF16)
     nf_ref[ep] = normed
-    gather = EpGather(nf_ref, nsend, nrecv, place)
-    gather.go(0, 1, 3, 2, 4)
+    rows = EpGather(nf_ref, fsend, frecv, place)
+    rows.go(0, 1, 3, 2, 4)
     logits = mm(wr_ref[...], normed, NT)
-    chosen = sel_ref[...] > 0.5
+    chosen = sel[...] > 0.5
     top = jnp.max(jnp.where(chosen, logits, MASKED), axis=0, keepdims=True)
     weight = jnp.where(chosen, jnp.exp(jnp.where(chosen, logits, MASKED) - top), 0.0)
     gates = weight / jnp.sum(weight, axis=0, keepdims=True)
@@ -505,11 +533,19 @@
         gscr[g] = gates[8 * g : 8 * g + 8, :]
     gin_ref[ep] = gscr[ep]
     exchange(gscr, gin_ref, gsend, grecv, place, False)
-    gather.whole()
+    exchange(slot_scr, slot_ref, ssend, srecv, place, True)
+    grads.got(0, 6, 8, 9, 10, 11, 12)
+    rows.whole()
     exchange(gscr, gin_ref, gsend, grecv, place, True)
-    gather.sent()
+    for g in (gather, grads, rows):
+        g.sent()
+    exchange_sent(slot_scr, slot_ref, ssend, srecv, place)
     exchange_sent(gscr, gin_ref, gsend, grecv, place)
-    exchange_sent(att_ref, abuf, asend, arecv, place)
+    repeat(1, 8, lambda r: piece_copy((ep + r) % 8).wait_send())
+    for g in range(4):
+        for h in (1, 2, 3):
+            for direction in (0, 1):
+                hop(direction, h, g, "sent")
 
 
 def each_slab(lead, work):
@@ -1414,52 +1450,37 @@
     layer_input, gain_attn, w_query, w_key, w_value, w_proj, gain_ffn, w_router,
     w_expert_in, w_expert_out, segment_ids, expert_ids, slot_order, out_grad,
 ):
-    ep = lax.axis_index("ep")
     gain_one, gain_two = gain_attn.reshape(1, 1024), gain_ffn.reshape(1, 1024)
     tables = [jnp.asarray(t) for t in rope_tables()]
-    w_own = jnp.concatenate(
-        [
-            lax.dynamic_slice_in_dim(w_query, ep * 128, 128, 1),
-            lax.dynamic_slice_in_dim(w_key, ep * 64, 64, 1),
-            lax.dynamic_slice_in_dim(w_value, ep * 64, 64, 1),
-        ],
-        axis=1,
-    )
     wr_rows = jnp.pad(w_router.T.reshape(8, 4, 1024), ((0, 0), (0, 4), (0, 0))).reshape(64, 1024)
     order = slot_order.reshape(TOK, 8)
     docs = segment_ids.reshape(32, 128)
 
-    normed_all, query, kv, grad_all, slots, chosen, starts = call(
-        first_kernel,
+    vm, hbm = pl.BlockSpec(memory_space=pltpu.VMEM), pl.BlockSpec(memory_space=pl.ANY)
+    wide, block = pltpu.VMEM((8, TOK, 1024), BF16), pltpu.VMEM((8, TOK, 128), BF16)
+    (
+        normed_all, grad_all, query, kv, slots, starts, attended_tall, log_sums, residual, ffn_all, gates_in, gates,
+    ) = call(
+        head_kernel,
         [
-            ((8, TOK, 1024), BF16), ((8, TOK, 128), BF16), ((8, 4, TOK, 128), BF16), ((8, TOK, 1024), BF16),
-            ((8, 8, TOK), F32), ((64, TOK), F32), ((32, 128), F32),
+            ((8, TOK, 1024), BF16), ((8, TOK, 1024), BF16), ((8, TOK, 128), BF16), ((8, 4, TOK, 128), BF16),
+            ((8, 8, TOK), F32), ((32, 128), F32), ((8, 128, TOK), F32), ((8, 8, 256), F32),
+            ((TOK, 1024), F32), ((8, TOK, 1024), BF16), ((8, 8, TOK), F32), ((64, TOK), F32),
         ],
-        [pltpu.VMEM((8, 8, TOK), F32)] + sems(13, 13, 13, 13, 8, 8, 24, 24),
-        [layer_input, gain_one, out_grad, w_own, *tables, expert_ids, expert_ids.T, order, order.T, docs],
-        "first", 1,
+        [
+            pltpu.VMEM((1024, 128), BF16), pltpu.VMEM((1024, 128), BF16), pltpu.VMEM((1024, 128), BF16),
+            pltpu.VMEM((1024, 256), BF16), pltpu.VMEM((1024, 1024), BF16), pltpu.VMEM((8, 8, TOK), F32),
+            pltpu.VMEM((64, TOK), F32), block, block, pltpu.VMEM((4096, 128), BF16), pltpu.VMEM((128, 4096), BF16),
+            pltpu.VMEM((8, 8, TOK), F32),
+        ]
+        + sems(4, 13, 13, 13, 13, 8, 8, 24, 24, 8, 8, 13, 13, 8, 8),
+        [
+            layer_input, gain_one, gain_two, out_grad, *tables, expert_ids.T, order.T, docs, wr_rows,
+            w_query, w_key, w_value, w_proj,
+        ],
+        "head", 1, in_specs=[vm] * 12 + [hbm] * 4,
     )
     kv_rows = kv.reshape(4096, 128)
-    ctx = lax.axis_index("ctx")
-    first = lax.dynamic_slice_in_dim(starts.reshape(8, 4, 128), ctx, 1, 1)[:, 0, 0].astype(jnp.int32) // CHUNK
-
-    vm, sm = pl.BlockSpec(memory_space=pltpu.VMEM), pl.BlockSpec(memory_space=pltpu.SMEM)
-    attended, attended_tall, log_sums = call(
-        attend_kernel,
-        [((8, TOK, 128), BF16), ((8, 128, TOK), F32), ((8, 8, 256), F32)],
-        [pltpu.VMEM((128, 4096), BF16)],
-        [first, query, kv_rows, starts],
-        "attend", in_specs=[sm, vm, vm, vm],
-    )
-    residual, ffn_all, gates_in, gates = call(
-        middle_kernel,
-        [((TOK, 1024), F32), ((8, TOK, 1024), BF16), ((8, 8, TOK), F32), ((64, TOK), F32)],
-        [pltpu.VMEM((8, TOK, 128), BF16), pltpu.VMEM((8, 8, TOK), F32)] + sems(8, 8, 13, 13, 8, 8),
-        [attended, layer_input, gain_two, w_proj, wr_rows, chosen],
-        "middle", 2,
-    )
-    hbm = pl.BlockSpec(memory_space=pl.ANY)
-    wide = pltpu.VMEM((8, TOK, 1024), BF16)
     ex, ez = len(X_FIRST), len(Z_FIRST)
     sums, back, grad_gates, sums_x, sums_z, units = call(
         expert_kernel,
@@ -1478,7 +1499,6 @@
         "experts", 4, in_specs=[vm, vm] + [hbm] * 4, out_specs=[vm] * 5 + [hbm],
     )
     nx, nz = len(X_UNITS), len(Z_UNITS)
-    block = pltpu.VMEM((8, TOK, 128), BF16)
 
     def direct(lanes):
         return [

time: 250 us -> 233 us (0.932)
  Pallas kernels: 238 us -> 226 us
  local copies, waits for them, and re-layouts: 8.46 us -> 4.02 us
    pallas_call x6 -> x4, Pallas kernels: 238 us -> 226 us  [call(): pl.pallas_call(kernel, out_shape=[jax.ShapeDtypeStruct(shape, kind) for s...]
where the time goes in v1:
time: 233 us; the launch traced here: 232 us
  Pallas kernels  226 us (97%)
  local copies, waits for them, and re-layouts  4.02 us (2%)
    pallas_call x4, Pallas kernels, call(): pl.pallas_call(kernel, out_shape=[jax.ShapeDtypeStruct(shape, kind) for s...  226 us

profile of v1, /device:TPU:8, one launch (start us, length us, event | category | flops | bytes accessed | tf_op | source)
XLA Modules:
  0.0 232.4 jit_solution(5893848558706877851)
XLA Ops:
  0.6 0.5 broadcast.5
  1.2 1.3 reduce.3
  2.5 0.1 reshape.45
  2.6 0.7 copy.29
  3.3 0.9 reshape.47
  4.1 0.7 pad_bitcast_fusion.wr_ref
  4.8 70.8 %head.1 = (bf16[8,128,1024]{2,1,0:T(8,128)(2,1)}, bf16[8,128,1024]{2,1,0:T(8,128)(2,1)}, bf16[8,128,128]{2,1,0:T(8,128)(2,1)}, bf16[8,4,128,128]{3,2,1,0:T(8,128...) custom-call(bf16[128,1024]{1,0:T(8,128)(2,1)} %x_ref.3, ...), custom_call_target="tpu_custom_call" | custom-call | tf_op jit(solution)/shard_map/head/pallas_call | solution.py:1433
  75.6 38.3 %experts.1 = (bf16[8,128,1024]{2,1,0:T(8,128)(2,1)}, bf16[8,128,1024]{2,1,0:T(8,128)(2,1)}, f32[8,8,128]{2,1,0:T(8,128)}, bf16[8,2,16,1024]{3,2,1,0:T(8,128)(2,1...) custom-call(f32[8,8,128]{2,1,0:T(8,128)} %get-tuple-element.49.slot_ref, ...), custom_call_target="tpu_custom_call" | custom-call | tf_op jit(solution)/shard_map/experts/pallas_call | solution.py:1433
  113.9 114.8 %tail.1 = (bf16[128,1024]{1,0:T(8,128)(2,1)}, bf16[128,1024]{1,0:T(8,128)(2,1)}, f32[4,32,1024]{2,1,0:T(8,128)}, f32[4,16,1024]{2,1,0:T(8,128)}, f32[4,1024]{1,0...) custom-call(f32[8,8,128]{2,1,0:T(8,128)} %get-tuple-element.53.dg_re, ...), custom_call_target="tpu_custom_call" | custom-call | tf_op jit(solution)/shard_map/tail/pallas_call | solution.py:1433
  228.8 2.5 %pack.1 = (bf16[128,1024]{1,0:T(8,128)(2,1)}, bf16[128,1024]{1,0:T(8,128)(2,1)}, f32[4,32,1024]{2,1,0:T(8,128)}, f32[4,16,1024]{2,1,0:T(8,128)}, f32[4,1024]{1,0...) custom-call(bf16[128,1024]{1,0:T(8,128)(2,1)} %get-tuple-element.67., ...), custom_call_target="tpu_custom_call" | custom-call | tf_op jit(solution)/shard_map/pack/pallas_call | solution.py:1433
  231.2 1.2 slice_bitcast_fusion

commit v2 on v1

--- a/solution.py
+++ b/solution.py
@@ -261,14 +261,31 @@
     return jnp.maximum(value, above)
 
 
-def slots_of(eidT_ref, soT_ref, slot_scr, sel_ref):
+def priorities(order):
+    def spread(part):
+        return mm(part.astype(F32).astype(BF16), from_rows, TN)
+
+    r = lax.broadcasted_iota(jnp.int32, (8, 128), 0)
+    t = lax.broadcasted_iota(jnp.int32, (8, 128), 1)
+    from_rows = jnp.where(t // 16 == r, 1.0, 0.0).astype(BF16)
+    of_k = jnp.where(t % 8 == r, 1.0, 0.0).astype(BF16)
+    l = lax.broadcasted_iota(jnp.int32, (128, 128), 0)
+    t = lax.broadcasted_iota(jnp.int32, (128, 128), 1)
+    meets = l // 8 == t % 16
+    high = jnp.where(meets, spread(order // 32), 0.0).astype(BF16)
+    low = jnp.where(meets, spread(order % 32), 0.0).astype(BF16)
+    return mm(of_k, high) * 32.0 + mm(of_k, low)
+
+
+def slots_of(eidT_ref, order_ref, slot_scr, sel_ref):
     def expert(index):
         return jnp.where(index % 8 < 4, (index // 8) * 4 + index % 8, -1)
 
     row_expert = expert(lax.broadcasted_iota(jnp.int32, (64, TOK), 0))
     by_row = jnp.full((64, TOK), BIG, F32)
+    ranks = priorities(order_ref[...])
     for k in range(8):
-        by_row = jnp.where(eidT_ref[k : k + 1, :] == row_expert, soT_ref[k : k + 1, :].astype(F32), by_row)
+        by_row = jnp.where(eidT_ref[k : k + 1, :] == row_expert, ranks[k : k + 1, :], by_row)
     by_lane = by_row.T
     sel_ref[...] = jnp.where(by_row < BIG, 1.0, 0.0)
     for g in range(8):
@@ -284,8 +301,8 @@
 CHUNK = 512
 
 
-def key_mask(chunk, start_row, place_row):
-    keys = (lax.broadcasted_iota(jnp.int32, (CHUNK, 256), 0) + chunk * CHUNK).astype(F32)
+def key_mask(step, start_row, place_row):
+    keys = (lax.broadcasted_iota(jnp.int32, (2 * CHUNK, 256), 0) + step * (2 * CHUNK)).astype(F32)
     return (keys >= start_row) & (keys <= place_row)
 
 
@@ -305,7 +322,7 @@
 
 
 def head_kernel(
-    x_ref, gain_one_ref, gain_two_ref, og_ref, ca_ref, sa_ref, cb_ref, sb_ref, eidT_ref, soT_ref, doc_ref, wr_ref,
+    x_ref, gain_one_ref, gain_two_ref, og_ref, ca_ref, sa_ref, cb_ref, sb_ref, eidT_ref, order_ref, doc_ref, wr_ref,
     wq_hbm, wk_hbm, wv_hbm, wp_hbm,
     nall_ref, ogall_ref, q_ref, kv_ref, slot_ref, start_ref, attT_ref, lse_ref, res_ref, nf_ref, gin_ref, gates_ref,
     wq, wk, wv, w_own, wp, slot_scr, sel, att, abuf, kv_rows, kvT, gscr,
@@ -412,7 +429,7 @@
     project(0)
     hops(1, 0)
     start_ref[...] = starts_of(doc_ref[...])
-    slots_of(eidT_ref, soT_ref, slot_scr, sel)
+    slots_of(eidT_ref, order_ref, slot_scr, sel)
     gather.got(1)
     gather.go(5, 6)
     gather.got(3)
@@ -471,17 +488,17 @@
         wide = heads_wide(turned(q_ref[j]))
         q_pad = jnp.concatenate([wide, jnp.zeros_like(wide)], axis=0)
 
-        def step(chunk, carry):
+        def step(i, carry):
             top, total = carry
-            rows = pl.ds(pl.multiple_of(chunk * CHUNK, CHUNK), CHUNK)
+            rows = pl.ds(pl.multiple_of(i * (2 * CHUNK), 2 * CHUNK), 2 * CHUNK)
             scores = mm(kv_rows[rows, :], q_pad)
-            scores = jnp.where(key_mask(chunk, start_row, place_row), scores, MASKED)
+            scores = jnp.where(key_mask(i, start_row, place_row), scores, MASKED)
             new_top = jnp.maximum(top, jnp.max(scores, axis=0, keepdims=True))
             probs = jnp.exp(scores - new_top).astype(BF16)
             total = total * jnp.exp(top - new_top) + mm(kvT[:, rows], probs)
             return new_top, total
 
-        top, total = lax.fori_loop(0, j + 1, step, (jnp.full((1, 256), MASKED, F32), jnp.zeros((128, 256), F32)))
+        top, total = lax.fori_loop(0, j // 2 + 1, step, (jnp.full((1, 256), MASKED, F32), jnp.zeros((128, 256), F32)))
         norm = total[0:1]
         out = total[HD:] / norm
         tall = jnp.concatenate([out[:, :128], out[:, 128:]], axis=0)
@@ -523,7 +540,10 @@
     nf_ref[ep] = normed
     rows = EpGather(nf_ref, fsend, frecv, place)
     rows.go(0, 1, 3, 2, 4)
-    logits = mm(wr_ref[...], normed, NT)
+    to = lax.broadcasted_iota(jnp.int32, (64, 32), 0)
+    source = lax.broadcasted_iota(jnp.int32, (64, 32), 1)
+    spread = jnp.where((to % 8 < 4) & (source == (to // 8) * 4 + to % 8), 1.0, 0.0).astype(BF16)
+    logits = mm(mm(spread, wr_ref[...]).astype(BF16), normed, NT)
     chosen = sel[...] > 0.5
     top = jnp.max(jnp.where(chosen, logits, MASKED), axis=0, keepdims=True)
     weight = jnp.where(chosen, jnp.exp(jnp.where(chosen, logits, MASKED) - top), 0.0)
@@ -928,7 +948,7 @@
     dg_ref, gates_ref, gain_two_ref, wr_ref, x_ref, gain_one_ref, ca_ref, sa_ref, cb_ref, sb_ref, start_ref, lse_ref,
     rx0, rz0,
     back_hbm, nf_hbm, res_hbm, og_hbm, q_hbm, kv_hbm, attT_hbm, wp_hbm, y_hbm, nall_hbm, wq_hbm, wk_hbm, wv_hbm, gw_hbm,
-    out_ref, ing_ref, gin_ref, gout_ref, gq_ref, gk_ref, gv_ref, gside_ref, gproj_out, gains_ref,
+    out_ref, ing_ref, gin_ref, gout_ref, gq_ref, gk_ref, gv_ref, gproj_out, gside_ref, gains_ref,
     back, nf, res, og, q_ref, kv, attT, wp, y_part, wq, wk, wv, own,
     dbuf, cbuf, fbuf, gbuf, cbuf2, fbuf2, gbuf2, gm, gres,
     kT, both, stack, rows, dqs, acc, dkv, dqb, dkvb, kbuf, qpieces, kpieces,
@@ -1040,6 +1060,10 @@
     grad_logits = gates * (grad_gates - jnp.sum(gates * grad_gates, axis=0, keepdims=True))
     high = grad_logits.astype(BF16)
     low = (grad_logits - high.astype(F32)).astype(BF16)
+    to = lax.broadcasted_iota(jnp.int32, (32, 64), 0)
+    source = lax.broadcasted_iota(jnp.int32, (32, 64), 1)
+    squeeze = jnp.where(source == (to // 4) * 8 + to % 4, 1.0, 0.0).astype(BF16)
+    high, low = mm(squeeze, high).astype(BF16), mm(squeeze, low).astype(BF16)
     from_router = mm(high, wr_ref[...], TN) + mm(low, wr_ref[...], TN)
     resid = res[...]
     scale = lax.rsqrt(jnp.mean(resid * resid, axis=-1, keepdims=True) + EPSILON)
@@ -1085,10 +1109,7 @@
     gather.got(7)
     gather.go(12)
     g0.advance(4)
-    to = lax.broadcasted_iota(jnp.int32, (32, 64), 0)
-    source = lax.broadcasted_iota(jnp.int32, (32, 64), 1)
-    squeeze = jnp.where(source == (to // 4) * 8 + to % 4, 1.0, 0.0).astype(BF16)
-    grad_router = mm(mm(squeeze, high).astype(BF16), nf[...]) + mm(mm(squeeze, low).astype(BF16), nf[...])
+    grad_router = mm(high, nf[...]) + mm(low, nf[...])
     side = jnp.concatenate([grad_router, jnp.zeros((96, 1024), F32)], axis=0)
     for d in range(8):
         tile = side[:, d * 128 : (d + 1) * 128].T.astype(BF16)
@@ -1241,6 +1262,9 @@
     chunk_done(7)
     weights(dkvb[...], late_k)
     sums_k.start()
+    for i in (4, 5, 6):
+        finish_x(i)
+    g2.start()
     pieces_got(dqb, qpieces, qsend, qrecv)
     grad_q = jnp.concatenate([qpieces[p] for p in range(8)], axis=1)
     grad_normed = mm(grad_q, wq[...], NT)
@@ -1324,17 +1348,18 @@
         repeat(1, count + 1, lambda r: gain_copy(stage, r).start())
 
     gain_stage(0, 7)
+    g2.advance(2)
     grad_normed = grad_normed * gain_one_ref[...]
     mean = jnp.mean(grad_normed * scaled, axis=-1, keepdims=True)
     ing_ref[...] = (gres[...] + scale * (grad_normed - scaled * mean)).astype(BF16)
 
     sums_q.turn()
     gain_stage(1, 3)
+    g2.advance(3)
     sums_k.turn()
-    for i in (4, 5, 6):
-        finish_x(i)
-    g2.start()
     gain_stage(2, 7)
+    g1.advance(4)
+    g2.advance(4)
 
     done_q, done_k = sums_q.finish(), sums_k.finish()
     for g in range(4):
@@ -1343,8 +1368,6 @@
         fin_late[g, :, 128:256] = done_k[at]
     each_piece((2,), lambda c: c.start(), True)
 
-    g1.advance(4)
-    g2.advance(2)
 
     def put_unit(unit, value):
         j, u = unit // 3, unit % 3
@@ -1368,7 +1391,6 @@
         gout_ref[0, :, 512 * h : 512 * h + 512] = value
     finish_units(h1, Z_UNITS)
     finish_units(g0, X_FIRST)
-    g2.advance(3)
     finish_units(g1, X_UNITS[:4])
     pieces_in(0)
     pieces_in(1)
@@ -1378,7 +1400,6 @@
         last = last + gain_z[r]
     gain_own[3] = last
 
-    g2.advance(4)
     pieces_in(2)
     odd = ctx % 2 == 1
 
@@ -1420,9 +1441,14 @@
 
 
 def pack_kernel(*refs):
-    count = len(refs) // 2
-    for src, dst in zip(refs[:count], refs[count:]):
+    count = (len(refs) - 1) // 2
+    for src, dst in zip(refs[: count - 2], refs[count:]):
         dst[...] = src[...]
+    side, gains = refs[count - 2 : count]
+    router, one, two = refs[-3:]
+    router[...] = side[:, 0:32]
+    one[...] = gains[0, 0:4]
+    two[...] = gains[8, 0:4]
 
 
 def call(kernel, outs, scratch, args, name, collective=None, **more):
@@ -1452,8 +1478,8 @@
 ):
     gain_one, gain_two = gain_attn.reshape(1, 1024), gain_ffn.reshape(1, 1024)
     tables = [jnp.asarray(t) for t in rope_tables()]
-    wr_rows = jnp.pad(w_router.T.reshape(8, 4, 1024), ((0, 0), (0, 4), (0, 0))).reshape(64, 1024)
-    order = slot_order.reshape(TOK, 8)
+    wr_rows = w_router.T
+    order = slot_order.reshape(8, 128)
     docs = segment_ids.reshape(32, 128)
 
     vm, hbm = pl.BlockSpec(memory_space=pltpu.VMEM), pl.BlockSpec(memory_space=pl.ANY)
@@ -1475,7 +1501,7 @@
         ]
         + sems(4, 13, 13, 13, 13, 8, 8, 24, 24, 8, 8, 13, 13, 8, 8),
         [
-            layer_input, gain_one, gain_two, out_grad, *tables, expert_ids.T, order.T, docs, wr_rows,
+            layer_input, gain_one, gain_two, out_grad, *tables, expert_ids.T, order, docs, wr_rows,
             w_query, w_key, w_value, w_proj,
         ],
         "head", 1, in_specs=[vm] * 12 + [hbm] * 4,
@@ -1509,7 +1535,7 @@
         tail_kernel,
         [
             ((TOK, 1024), BF16), ((TOK, 1024), BF16), ((4, 32, 1024), F32), ((4, 16, 1024), F32), ((4, 1024), F32),
-            ((4, 512), F32), ((4, 512), F32), ((4, 128), F32), ((4, 1024), F32), ((16, 128), F32),
+            ((4, 512), F32), ((4, 512), F32), ((4, 1024), F32), ((4, 128), F32), ((16, 128), F32),
         ],
         [
             wide, pltpu.VMEM((TOK, 1024), BF16), pltpu.VMEM((TOK, 1024), F32), pltpu.VMEM((TOK, 1024), BF16), block,
@@ -1551,12 +1577,11 @@
         ],
         "tail", 3, in_specs=[vm] * 14 + [hbm] * 14,
     )
-    layer_output, input_grad, grad_in, grad_out, out_q, out_k, out_v, side, out_proj, gains = call(
-        pack_kernel, [(r.shape, r.dtype) for r in results], [], results, "pack"
+    layer_output, input_grad, grad_in, grad_out, out_q, out_k, out_v, out_proj, router, gain_a, gain_b = call(
+        pack_kernel,
+        [(r.shape, r.dtype) for r in results[:8]] + [((4, 32), F32), ((4,), F32), ((4,), F32)], [], results, "pack",
     )
-    return (
-        layer_output, input_grad, gains[0, :4], out_q, out_k, out_v, out_proj, gains[8, :4], side[:, :32], grad_in, grad_out,
-    )
+    return layer_output, input_grad, gain_a, out_q, out_k, out_v, out_proj, gain_b, router, grad_in, grad_out
 
 
 def solution(mesh):

time: 233 us -> 221 us (0.948)
  Pallas kernels: 226 us -> 219 us
  local copies, waits for them, and re-layouts: 4.02 us -> 0 us
    pallas_call x4, Pallas kernels: 226 us -> 219 us  [call(): pl.pallas_call(kernel, out_shape=[jax.ShapeDtypeStruct(shape, kind) for s...]
where the time goes in v2:
time: 221 us; the launch traced here: 219 us
  Pallas kernels  219 us (99%)
    pallas_call x4, Pallas kernels, call(): pl.pallas_call(kernel, out_shape=[jax.ShapeDtypeStruct(shape, kind) for s...  219 us

profile of v2, /device:TPU:8, one launch (start us, length us, event | category | flops | bytes accessed | tf_op | source)
XLA Modules:
  0.0 219.4 jit_solution(11566507161214018891)
XLA Ops:
  0.6 68.0 %head.1 = (bf16[8,128,1024]{2,1,0:T(8,128)(2,1)}, bf16[8,128,1024]{2,1,0:T(8,128)(2,1)}, bf16[8,128,128]{2,1,0:T(8,128)(2,1)}, bf16[8,4,128,128]{3,2,1,0:T(8,128...) custom-call(bf16[128,1024]{1,0:T(8,128)(2,1)} %x_ref.3, ...), custom_call_target="tpu_custom_call" | custom-call | tf_op jit(solution)/shard_map/head/pallas_call | solution.py:1459
  68.7 37.9 %experts.1 = (bf16[8,128,1024]{2,1,0:T(8,128)(2,1)}, bf16[8,128,1024]{2,1,0:T(8,128)(2,1)}, f32[8,8,128]{2,1,0:T(8,128)}, bf16[8,2,16,1024]{3,2,1,0:T(8,128)(2,1...) custom-call(f32[8,8,128]{2,1,0:T(8,128)} %get-tuple-element.50.slot_ref, ...), custom_call_target="tpu_custom_call" | custom-call | tf_op jit(solution)/shard_map/experts/pallas_call | solution.py:1459
  106.6 110.2 %tail.1 = (bf16[128,1024]{1,0:T(8,128)(2,1)}, bf16[128,1024]{1,0:T(8,128)(2,1)}, f32[4,32,1024]{2,1,0:T(8,128)}, f32[4,16,1024]{2,1,0:T(8,128)}, f32[4,1024]{1,0...) custom-call(f32[8,8,128]{2,1,0:T(8,128)} %get-tuple-element.54.dg_re, ...), custom_call_target="tpu_custom_call" | custom-call | tf_op jit(solution)/shard_map/tail/pallas_call | solution.py:1459
  216.8 2.4 %pack.1 = (bf16[128,1024]{1,0:T(8,128)(2,1)}, bf16[128,1024]{1,0:T(8,128)(2,1)}, f32[4,32,1024]{2,1,0:T(8,128)}, f32[4,16,1024]{2,1,0:T(8,128)}, f32[4,1024]{1,0...) custom-call(bf16[128,1024]{1,0:T(8,128)(2,1)} %get-tuple-element.68., ...), custom_call_target="tpu_custom_call" | custom-call | tf_op jit(solution)/shard_map/pack/pallas_call | solution.py:1459

commit v3 on v2

--- a/solution.py
+++ b/solution.py
@@ -682,7 +682,7 @@
 
 X_FIRST, Z_FIRST = (0, 1), (2,)
 KEPT = 3
-X_UNITS, Z_UNITS = (3, 4, 5, 6, 7, 8, 9), (10, 11)
+X_UNITS, Z_UNITS = (3, 4, 5, 6, 7, 8), (9, 10, 11)
 
 
 def unit_arcs(torus, own, x_units, z_units, x_slots, z_slots, xs, xr, zs, zr):
@@ -973,7 +973,7 @@
     }
     units = {u: pltpu.make_async_copy(gw_hbm.at[u - KEPT], own.at[i], usem.at[i]) for i, u in enumerate(X_UNITS + Z_UNITS)}
     loads["back"].start()
-    for u in (3, 10, 4, 11, 5, 6, 7, 8, 9):
+    for u in (3, 9, 4, 10, 5, 11, 6, 7, 8):
         units[u].start()
     for name in ("nf", "res", "og", "kv", "q", "attT", "wp"):
         loads[name].start()
@@ -1013,9 +1013,9 @@
     xa, za = unit_arcs(torus, own, X_UNITS, Z_UNITS, x_slots, z_slots, xs, xr, zs, zr)
     g0 = torus.z_arc(lambda t: rx0.at[t], first_or_last((1, 1)), g0_slots, g0s, g0r)
     g1 = torus.z_arc(lambda t: rx1.at[t], first_or_last((2, 2)), g1_slots, g1s, g1r)
-    g2 = torus.z_arc(lambda t: rx2.at[t], first_or_last((1, 2)), g2_slots, g2s, g2r)
+    g2 = torus.z_arc(lambda t: rx2.at[t], first_or_last((1, 1)), g2_slots, g2s, g2r)
     h0 = torus.x_arc(lambda t: rz0.at[t], first_or_last((1, 1)), h0_slots, h0s, h0r)
-    h1 = torus.x_arc(lambda t: rz1.at[t], first_or_last((1, 1)), h1_slots, h1s, h1r)
+    h1 = torus.x_arc(lambda t: rz1.at[t], first_or_last((1, 2)), h1_slots, h1s, h1r)
 
     def finish_x(i):
         target = rx1 if i < 4 else rx2
@@ -1040,7 +1040,7 @@
     for i in range(4):
         units[X_UNITS[i]].wait()
         xa[i].start()
-        if i < 2:
+        if i < 3:
             units[Z_UNITS[i]].wait()
             za[i].start()
     g0.start()
@@ -1051,6 +1051,7 @@
     total.near()
     h0.advance(2)
     xa[1].advance(2)
+    za[2].advance(2)
     g0.advance(2)
     exchange(dg_ref, dbuf, dsend, drecv, place, True)
     for name in ("nf", "res", "og"):
@@ -1083,6 +1084,7 @@
     for t in range(8):
         gain_own[0, 8 + t : 9 + t, :] = gain_two[:, 128 * t : 128 * t + 128]
     xa[3].advance(2)
+    za[2].advance(3)
     g0.advance(3)
 
     for name in ("kv", "q"):
@@ -1108,6 +1110,7 @@
     gather.go(11)
     gather.got(7)
     gather.go(12)
+    za[2].advance(4)
     g0.advance(4)
     grad_router = mm(high, nf[...]) + mm(low, nf[...])
     side = jnp.concatenate([grad_router, jnp.zeros((96, 1024), F32)], axis=0)
@@ -1115,7 +1118,7 @@
         tile = side[:, d * 128 : (d + 1) * 128].T.astype(BF16)
         for c in range(4):
             early[d // 4, d % 4, c, :, 128:256] = tile[32 * c : 32 * c + 32]
-    for i in (4, 5, 6):
+    for i in (4, 5):
         units[X_UNITS[i]].wait()
         xa[i].start()
     for name in ("attT", "wp"):
@@ -1195,6 +1198,7 @@
         def _():
             finish_x(1)
             finish_z(1)
+            finish_z(2)
             results.near()
 
         @pl.when(m == 2)
@@ -1213,7 +1217,6 @@
         @pl.when(m == 4)
         def _():
             h1.advance(2)
-            xa[6].advance(2)
             out_ref[...] = (res[...] + results.last()).astype(BF16)
 
         @pl.when(m == 6)
@@ -1262,12 +1265,13 @@
     chunk_done(7)
     weights(dkvb[...], late_k)
     sums_k.start()
-    for i in (4, 5, 6):
+    for i in (4, 5):
         finish_x(i)
     g2.start()
     pieces_got(dqb, qpieces, qsend, qrecv)
     grad_q = jnp.concatenate([qpieces[p] for p in range(8)], axis=1)
     grad_normed = mm(grad_q, wq[...], NT)
+    sums_q.turn()
 
     def piece(g, h, kind, device):
         index = (kind * 4 + g) * 2 + h
@@ -1309,11 +1313,6 @@
 
         repeat(0, 8, one)
 
-    done_early = sums_early.finish()
-    for g in range(4):
-        fin[g] = done_early[8 * g : 8 * g + 8]
-    each_piece((0, 1), lambda c: c.start(), True)
-    g1.advance(3)
     for name in ("wk", "wv"):
         loads[name].wait()
     pieces_got(dkvb, kpieces, psend, precv)
@@ -1348,18 +1347,19 @@
         repeat(1, count + 1, lambda r: gain_copy(stage, r).start())
 
     gain_stage(0, 7)
+    sums_k.turn()
     g2.advance(2)
     grad_normed = grad_normed * gain_one_ref[...]
     mean = jnp.mean(grad_normed * scaled, axis=-1, keepdims=True)
     ing_ref[...] = (gres[...] + scale * (grad_normed - scaled * mean)).astype(BF16)
 
-    sums_q.turn()
     gain_stage(1, 3)
+    g1.advance(3)
+    done_early = sums_early.finish()
+    for g in range(4):
+        fin[g] = done_early[8 * g : 8 * g + 8]
+    each_piece((0, 1), lambda c: c.start(), True)
     g2.advance(3)
-    sums_k.turn()
-    gain_stage(2, 7)
-    g1.advance(4)
-    g2.advance(4)
 
     done_q, done_k = sums_q.finish(), sums_k.finish()
     for g in range(4):
@@ -1367,6 +1367,9 @@
         fin_late[g, :, 0:128] = done_q[at]
         fin_late[g, :, 128:256] = done_k[at]
     each_piece((2,), lambda c: c.start(), True)
+    gain_stage(2, 7)
+    g1.advance(4)
+    g2.advance(4)
 
 
     def put_unit(unit, value):
@@ -1552,9 +1555,9 @@
             pltpu.VMEM((8, 4, TOK, 128), BF16),
             block, block, pltpu.VMEM((8, 4, TOK, 128), BF16), block, block,
             pltpu.VMEM((nx, 2, 2, 2, 4, 16, 1024), BF16), pltpu.VMEM((nz, 2, 4, 4, 16, 1024), BF16),
-            pltpu.VMEM((2, 4, ex, 16, 1024), BF16), pltpu.VMEM((2, 4, 4, 16, 1024), BF16), pltpu.VMEM((2, 4, 3, 16, 1024), BF16),
+            pltpu.VMEM((2, 4, ex, 16, 1024), BF16), pltpu.VMEM((2, 4, 4, 16, 1024), BF16), pltpu.VMEM((2, 4, 2, 16, 1024), BF16),
             pltpu.VMEM((2, 2, 2, 16, 512), BF16), pltpu.VMEM((2, 2, nz, 16, 1024), BF16),
-            pltpu.VMEM((8, 4, 16, 1024), BF16), pltpu.VMEM((8, 3, 16, 1024), BF16), pltpu.VMEM((4, nz, 16, 1024), BF16),
+            pltpu.VMEM((8, 4, 16, 1024), BF16), pltpu.VMEM((8, 2, 16, 1024), BF16), pltpu.VMEM((4, nz, 16, 1024), BF16),
             pltpu.VMEM((2, 4, 4, 32, 256), BF16), pltpu.VMEM((2, 4, 4, 32, 128), BF16), pltpu.VMEM((2, 4, 4, 32, 128), BF16),
         ]
         + direct(256) + direct(128) + direct(128)

time: 221 us -> 217 us (0.982)
  Pallas kernels: 219 us -> 215 us
    pallas_call x4, Pallas kernels: 219 us -> 215 us  [call(): pl.pallas_call(kernel, out_shape=[jax.ShapeDtypeStruct(shape, kind) for s...]
where the time goes in v3:
time: 217 us; the launch traced here: 216 us
  Pallas kernels  215 us (99%)
    pallas_call x4, Pallas kernels, call(): pl.pallas_call(kernel, out_shape=[jax.ShapeDtypeStruct(shape, kind) for s...  215 us

profile of v3, /device:TPU:8, one launch (start us, length us, event | category | flops | bytes accessed | tf_op | source)
XLA Modules:
  0.0 215.6 jit_solution(13463894571238499658)
XLA Ops:
  0.6 68.0 %head.1 = (bf16[8,128,1024]{2,1,0:T(8,128)(2,1)}, bf16[8,128,1024]{2,1,0:T(8,128)(2,1)}, bf16[8,128,128]{2,1,0:T(8,128)(2,1)}, bf16[8,4,128,128]{3,2,1,0:T(8,128...) custom-call(bf16[128,1024]{1,0:T(8,128)(2,1)} %x_ref.3, ...), custom_call_target="tpu_custom_call" | custom-call | tf_op jit(solution)/shard_map/head/pallas_call | solution.py:1462
  68.7 37.9 %experts.1 = (bf16[8,128,1024]{2,1,0:T(8,128)(2,1)}, bf16[8,128,1024]{2,1,0:T(8,128)(2,1)}, f32[8,8,128]{2,1,0:T(8,128)}, bf16[8,2,16,1024]{3,2,1,0:T(8,128)(2,1...) custom-call(f32[8,8,128]{2,1,0:T(8,128)} %get-tuple-element.50.slot_ref, ...), custom_call_target="tpu_custom_call" | custom-call | tf_op jit(solution)/shard_map/experts/pallas_call | solution.py:1462
  106.6 106.4 %tail.1 = (bf16[128,1024]{1,0:T(8,128)(2,1)}, bf16[128,1024]{1,0:T(8,128)(2,1)}, f32[4,32,1024]{2,1,0:T(8,128)}, f32[4,16,1024]{2,1,0:T(8,128)}, f32[4,1024]{1,0...) custom-call(f32[8,8,128]{2,1,0:T(8,128)} %get-tuple-element.54.dg_re, ...), custom_call_target="tpu_custom_call" | custom-call | tf_op jit(solution)/shard_map/tail/pallas_call | solution.py:1462
  213.0 2.4 %pack.1 = (bf16[128,1024]{1,0:T(8,128)(2,1)}, bf16[128,1024]{1,0:T(8,128)(2,1)}, f32[4,32,1024]{2,1,0:T(8,128)}, f32[4,16,1024]{2,1,0:T(8,128)}, f32[4,1024]{1,0...) custom-call(bf16[128,1024]{1,0:T(8,128)(2,1)} %get-tuple-element.68., ...), custom_call_target="tpu_custom_call" | custom-call | tf_op jit(solution)/shard_map/pack/pallas_call | solution.py:1462
